TPU v7x, 32 devices: a whole 2x2x4 slice. The times are simulated.
32 devices in a mesh: su: 8 (over z, core), sv: 2 (over x), nrm: 2 (over y).
Axes of the slice: x: 2, y: 2, z: 4, core: 2. Of those that a mesh axis runs over, the one named last changes fastest.
Arguments:
- primitive: float32 [5, 128, 80, 256], P(None, 'su', 'sv', 'nrm'), may hold values from -4 to 4, as said below
- adjoint_state: float32 [5, 128, 80, 256], P(None, 'su', 'sv', 'nrm'), may hold values from -0.6 to 0.6
- objective_grad: float32 [5, 128, 80, 256], P(None, 'su', 'sv', 'nrm'), may hold values from -6 to 6
- front_height: float32 [128, 80], P('su', 'sv'), may hold values from 0.8 to 1.25
- shock_state: float32 [5, 128, 80], P(None, 'su', 'sv'), may hold values from -4 to 4, as said below
- state_by_height: float32 [5, 128, 80], P(None, 'su', 'sv'), may hold values from -18 to 18
- state_by_slope: float32 [5, 128, 80], P(None, 'su', 'sv'), may hold values from -6 to 6
- fitted_flags: int32 [128, 80], P('su', 'sv'), may hold values 0 or 1
Outputs:
- adjoint_residual: float32 [5, 128, 80, 256], P(None, 'su', 'sv', 'nrm')
- slope_sensitivity: float32 [128, 80], P('su', 'sv')
Inputs may be any that keep to these rules, and one draw needn't show every extreme that they name: `primitive`: variables 0 (density) and 4 (pressure) lie in 0.5 to 2; variables 1 to 3 are velocity components. `shock_state`: variables 0 (density) and 4 (pressure) lie in 0.5 to 2; variables 1 to 3 are velocity components.
All inputs are finite; a program needn't handle non-finite values. No bound on the sum of `fitted_flags` on one device may be relied on, other than what follows from the above.
Results may differ from a plain program's by a relative error of at most 0.0003.
Values sent between devices are 32-bit elements; how exact they have to be, the bound alone decides.
A program may use at most 128 MiB of HBM per device.

v0:
```python
import jax
import jax.numpy as jnp
from jax import lax
from jax.sharding import PartitionSpec as P

gamma_ratio = 1.4
damping_coef = 0.0625
stretch_rate = 2.2


def prefix(part, axis, combine, identity):
    count = lax.axis_size(axis)
    place = lax.axis_index(axis)
    ahead = count - 1 - place
    gathered = lax.all_gather(part, axis)
    state = jnp.zeros_like(part) + jnp.asarray(identity, part.dtype)

    def one(lap, state):
        source = count - 1 - lap
        return combine(state, lax.dynamic_index_in_dim(gathered, source, 0, False))

    return lax.fori_loop(0, ahead, one, state)


def extended(block, sides, width):
    for axis, dim in sides:
        count = lax.axis_size(axis)
        forward = [(i, i + 1) for i in range(count - 1)]
        backward = [(target, source) for source, target in forward]
        low = lax.ppermute(
            lax.slice_in_dim(block, block.shape[dim] - width, None, axis=dim), axis, forward
        )
        high = lax.ppermute(lax.slice_in_dim(block, 0, width, axis=dim), axis, backward)
        block = jnp.concatenate([low, block, high], axis=dim)
    return block


def spread(block, axis, source):
    block = jnp.where(lax.axis_index(axis) == source, block, jnp.zeros_like(block))
    return lax.psum(block, axis)


def thermo(state):
    speed_square = state[1] * state[1] + state[2] * state[2] + state[3] * state[3]
    kinetic = 0.5 * (gamma_ratio - 1.0) * speed_square
    enthalpy = gamma_ratio * state[4] / ((gamma_ratio - 1.0) * state[0]) + 0.5 * speed_square
    return (kinetic, enthalpy)


def line_flux(state, enthalpy):
    mass_flow = state[0] * state[3]
    return jnp.stack(
        [
            mass_flow,
            mass_flow * state[1],
            mass_flow * state[2],
            mass_flow * state[3] + state[4],
            mass_flow * enthalpy,
        ],
        0,
    )


def flux_transpose(state, kinetic, enthalpy, adjoint, direction):
    normal_speed = state[direction]
    projected = adjoint[direction]
    dotted = state[1] * adjoint[1] + state[2] * adjoint[2] + state[3] * adjoint[3]
    energy_term = adjoint[4]
    mass_row = (
        kinetic * projected
        - normal_speed * dotted
        + normal_speed * (kinetic - enthalpy) * energy_term
    )
    common = adjoint[0] + dotted + enthalpy * energy_term
    shared = projected + normal_speed * energy_term
    pieces = [mass_row]
    for component in (1, 2, 3):
        entry = normal_speed * adjoint[component] - (gamma_ratio - 1.0) * state[component] * shared
        if component == direction:
            entry = entry + common
        pieces.append(entry)
    pieces.append((gamma_ratio - 1.0) * projected + gamma_ratio * normal_speed * energy_term)
    return jnp.stack(pieces, 0)


def tangent_parts(padded_adjoint, padded_radius, along_axis, length):

    def window(source, offset):
        return lax.slice_in_dim(source, offset, offset + length, axis=along_axis)

    gradient = (
        8.0 * (window(padded_adjoint, 1) - window(padded_adjoint, 3))
        - (window(padded_adjoint, 0) - window(padded_adjoint, 4))
    ) / 12.0
    weighted = padded_radius[None] * padded_adjoint
    fourth = (
        window(weighted, 0)
        - 4.0 * window(weighted, 1)
        + 6.0 * window(weighted, 2)
        - 4.0 * window(weighted, 3)
        + window(weighted, 4)
    )
    return (gradient, fourth)


def add_totals(earlier, later):
    return earlier + later


def upstream_sum(column_totals):
    return prefix(column_totals, "su", add_totals, jnp.zeros_like(column_totals))


def local(
    primitive,
    adjoint_state,
    objective_grad,
    front_height,
    shock_state,
    state_by_height,
    state_by_slope,
    fitted_flags,
):
    row_count = adjoint_state.shape[1]
    column_count = adjoint_state.shape[2]
    line_depth = adjoint_state.shape[3]
    line_count = lax.axis_size("nrm")
    line_index = lax.axis_index("nrm")
    total_depth = line_depth * line_count
    position = (line_index * line_depth + jnp.arange(line_depth, dtype=jnp.int32)).astype(
        jnp.float32
    ) + 0.5
    fraction = position / total_depth
    stretch = jnp.exp(stretch_rate * (fraction - 1.0))
    kinetic, enthalpy = thermo(primitive)
    sound_speed = jnp.sqrt(gamma_ratio * primitive[4] / primitive[0])
    radius_first = jnp.abs(primitive[1]) + sound_speed
    radius_second = jnp.abs(primitive[2]) + sound_speed
    stacked = jnp.concatenate([adjoint_state, radius_first[None], radius_second[None]], 0)
    padded = extended(stacked, (("su", 1), ("sv", 2)), 2)
    first_pad = padded[:, :, 2 : column_count + 2]
    second_pad = padded[:, 2 : row_count + 2]
    first_grad, first_fourth = tangent_parts(first_pad[:5], first_pad[5], 1, row_count)
    second_grad, second_fourth = tangent_parts(second_pad[:5], second_pad[6], 2, column_count)
    scaled = adjoint_state / (2.0 * front_height[None, :, :, None] * stretch[None, None, None, :])
    fluxes = line_flux(primitive, enthalpy)
    line_pad = extended(jnp.concatenate([scaled, fluxes], 0), (("nrm", 3),), 1)
    on_front = line_index == line_count - 1
    shock_kinetic, shock_enthalpy = thermo(shock_state)
    shock_flux = line_flux(shock_state, shock_enthalpy)
    top_flux = jnp.where(on_front, shock_flux, line_pad[5:, :, :, line_depth + 1])
    flux_above = jnp.concatenate([line_pad[5:, :, :, 2 : line_depth + 1], top_flux[..., None]], -1)
    flux_below = line_pad[5:, :, :, 0:line_depth]
    metric_part = -jnp.sum(scaled * (flux_above - flux_below), axis=(0, 3)) / front_height
    normal_term = flux_transpose(
        primitive,
        kinetic,
        enthalpy,
        line_pad[:5, :, :, 0:line_depth] - line_pad[:5, :, :, 2 : line_depth + 2],
        3,
    )
    top_scaled = scaled[..., line_depth - 1]
    metric = lax.psum(metric_part, "nrm")
    shock_adjoint = flux_transpose(shock_state, shock_kinetic, shock_enthalpy, top_scaled, 3)
    fitted = fitted_flags.astype(jnp.float32)
    height_term = metric + fitted * jnp.sum(shock_adjoint * state_by_height, 0)
    local_total = lax.cumsum(height_term, axis=0, reverse=True)
    upstream = upstream_sum(local_total[0])
    surface_count = row_count * lax.axis_size("su")
    slope_sens = (local_total + upstream[None, :]) / surface_count + fitted * jnp.sum(
        shock_adjoint * state_by_slope, 0
    )
    slope_sens = spread(slope_sens, "nrm", line_count - 1)
    result = (
        objective_grad
        + flux_transpose(primitive, kinetic, enthalpy, first_grad, 1)
        + flux_transpose(primitive, kinetic, enthalpy, second_grad, 2)
        + damping_coef * (first_fourth + second_fourth)
        + normal_term
        + fraction[None, None, None, :] * slope_sens[None, :, :, None] * fluxes
    )
    return (result, slope_sens)


def solution(mesh):
    placed = (
        P(None, "su", "sv", "nrm"),
        P(None, "su", "sv", "nrm"),
        P(None, "su", "sv", "nrm"),
        P("su", "sv"),
        P(None, "su", "sv"),
        P(None, "su", "sv"),
        P(None, "su", "sv"),
        P("su", "sv"),
    )
    return jax.shard_map(
        local,
        mesh=mesh,
        in_specs=placed,
        out_specs=(P(None, "su", "sv", "nrm"), P("su", "sv")),
        check_vma=False,
    )
```

profile of v0, /device:TPU:0, one launch (start us, length us, event | category | flops | bytes accessed | tf_op | source)
XLA Modules:
  0.0 105.2 jit_solution(12746115682884157483)
XLA Ops:
  3.1 1.6 %copy-done.1 = f32[5,16,40,128]{3,2,1,0:T(8,128)S(1)} copy-done((f32[5,16,40,128]{3,2,1,0:T(8,128)S(1)}, f32[5,16,40,128]{3,2,1,0:T(8,128)}, u32[]{:S(2)}) %copy-start.1) | copy-done | bytes 1638424
  5.8 3.2 %collective-permute-start = (f32[7,2,40,128]{3,2,1,0:T(8,128)}, f32[7,2,40,128]{3,2,1,0:T(8,128)}, u32[]{:S(2)}, u32[]{:S(2)}) collective-permute-start(f32[7,2,40,128]{3,2,1,0:T(8,128)} %get-tuple-element.114), channel_id=1, source_target_pairs={{0,4},{4,8},{8,12},{12,16},{16,20},{20,24},{24,28},{1,5},{5,9},{9,... | collective-permute-start | bytes 860168 | tf_op jit(solution)/shard_map/ppermute | solution.py:30
  12.8 1.6 %collective-permute-done.1 = f32[7,2,40,128]{3,2,1,0:T(8,128)} collective-permute-done((f32[7,2,40,128]{3,2,1,0:T(8,128)}, f32[7,2,40,128]{3,2,1,0:T(8,128)}, u32[]{:S(2)}, u32[]{:S(2)}) %collective-permute-start.1) | collective-permute-done | bytes 286752 | tf_op jit(solution)/shard_map/ppermute | solution.py:33
  14.3 1.8 %maximum_maximum_fusion = (f32[7,18,40,128]{3,2,1,0:T(8,128)S(1)}, f32[7,18,40,128]{3,2,1,0:T(8,128)S(1)}) fusion(f32[1,16,40,128]{3,2,1,0:T(8,128)} %copy-done.6, f32[1,16,40,128]{3,2,1,0:T(8,128)} %copy-done.9, f32[5,16,40,128]{3,2,1,0:T(8,128)S(1)} %copy-done, f32[7,2,40,128]{3,2,1,0:T(8,128)} %collective-permute-done, ...), kind=kLoop, calls=%fused_computation.1 | loop fusion | flops 3870720 | bytes 8028160 | tf_op jit(solution)/shard_map/concatenate | solution.py:34
  16.5 2.2 %copy-done.4 = f32[10,16,40,128]{3,2,1,0:T(8,128)S(1)} copy-done((f32[10,16,40,128]{3,2,1,0:T(8,128)S(1)}, f32[10,16,40,128]{3,2,1,0:T(8,128)}, u32[]{:S(2)}) %copy-start.4) | copy-done | bytes 3276824
  20.8 3.9 %fusion.44 = (f32[10,16,40,1]{3,2,1,0:T(8,128)}, f32[10,16,40,1]{3,2,1,0:T(8,128)}) fusion(f32[10,16,40,128]{3,2,1,0:T(8,128)S(1)} %get-tuple-element.130), kind=kLoop, calls=%fused_computation.172 | loop fusion | bytes 102400 | tf_op jit(solution)/shard_map/slice | solution.py:31
  24.7 3.3 %copy.401 = f32[10,16,40,1]{2,1,3,0:T(8,128)} copy(f32[10,16,40,1]{3,2,1,0:T(8,128)} %get-tuple-element.106) | data formatting | bytes 51200 | tf_op jit(solution)/shard_map/slice | solution.py:31
  28.0 4.1 %collective-permute-start.4 = (f32[10,16,40,1]{2,1,3,0:T(8,128)}, f32[10,16,40,1]{2,1,3,0:T(8,128)}, u32[]{:S(2)}, u32[]{:S(2)}) collective-permute-start(f32[10,16,40,1]{2,1,3,0:T(8,128)} %copy.401), channel_id=1, source_target_pairs={{0,1},{2,3},{4,5},{6,7},{8,9},{10,11},{12,13},{14,15},{16,17},{18,... | collective-permute-start | bytes 76808 | tf_op jit(solution)/shard_map/ppermute | solution.py:30
  32.1 3.3 %copy.403 = f32[10,16,40,1]{2,1,3,0:T(8,128)} copy(f32[10,16,40,1]{3,2,1,0:T(8,128)} %get-tuple-element.107) | data formatting | bytes 51200 | tf_op jit(solution)/shard_map/slice | solution.py:33
  35.3 1.4 %collective-permute-start.5 = (f32[10,16,40,1]{2,1,3,0:T(8,128)}, f32[10,16,40,1]{2,1,3,0:T(8,128)S(1)}, u32[]{:S(2)}, u32[]{:S(2)}) collective-permute-start(f32[10,16,40,1]{2,1,3,0:T(8,128)} %copy.403), channel_id=1, source_target_pairs={{1,0},{3,2},{5,4},{7,6},{9,8},{11,10},{13,12},{15,14},{17,16},{19,... | collective-permute-start | bytes 76808 | tf_op jit(solution)/shard_map/ppermute | solution.py:33
  36.7 1.9 %pad_maximum_fusion.27 = (f32[7,20,2,128]{3,2,1,0:T(2,128)}, f32[7,20,2,128]{3,2,1,0:T(2,128)}) fusion(f32[7,2,40,128]{3,2,1,0:T(8,128)} %collective-permute-done.1, f32[7,2,40,128]{3,2,1,0:T(8,128)} %collective-permute-done, f32[1,16,40,128]{3,2,1,0:T(8,128)} %copy-done.6, f32[1,16,40,128]{3,2,1,0:T(8,128)} %copy-done.9, f32[5,16,40,128]{3,2,1,0:T(8,128)S(1)} %copy-done), kind=kLoop, calls=%fused_computation.121 | loop fusion | flops 286720 | bytes 3153920 | tf_op jit(solution)/shard_map/slice | solution.py:31
  38.6 3.4 %collective-permute-start.2 = (f32[7,20,2,128]{3,2,1,0:T(2,128)}, f32[7,20,2,128]{3,2,1,0:T(2,128)S(1)}, u32[]{:S(2)}, u32[]{:S(2)}) collective-permute-start(f32[7,20,2,128]{3,2,1,0:T(2,128)} %get-tuple-element.108), channel_id=1, source_target_pairs={{0,2},{1,3},{4,6},{5,7},{8,10},{9,11},{12,14},{13,15},{16,18},{17,... | collective-permute-start | bytes 430088 | tf_op jit(solution)/shard_map/ppermute | solution.py:30
  44.2 2.6 %fusion = f32[5,20,40,128]{3,2,1,0:T(8,128)} fusion(f32[7,2,40,128]{3,2,1,0:T(8,128)} %collective-permute-done.1, f32[7,2,40,128]{3,2,1,0:T(8,128)} %collective-permute-done, f32[1,16,40,128]{3,2,1,0:T(8,128)S(1)} %copy-done.7, f32[1,16,40,128]{3,2,1,0:T(8,128)S(1)} %copy-done.10, f32[5,16,40,128]{3,2,1,0:T(8,128)S(1)} %copy-done, ...), kind=kLoop, calls=%fused_computation.4 | loop fusion | flops 2560000 | bytes 5324800 | tf_op jit(solution)/shard_map/mul | solution.py:95
  46.8 1.7 %slice.386 = f32[5,16,40,127]{3,2,1,0:T(8,128)} slice(f32[5,16,40,128]{3,2,1,0:T(8,128)S(1)} %copy-done.21), slice={[0:5], [0:16], [0:40], [1:128]} | slice | bytes 3251200 | tf_op jit(solution)/shard_map/slice | solution.py:152
  48.5 1.8 %copy.406 = f32[5,16,40,1]{3,2,1,0:T(8,128)} copy(f32[5,16,40,1]{2,1,3,0:T(8,128)S(1)} %slice_select_fusion) | data formatting | bytes 25600 | tf_op jit(solution)/shard_map/jit(_where)/select_n | solution.py:151
  50.3 2.5 %copy.404 = f32[10,16,40,1]{3,2,1,0:T(8,128)} copy(f32[10,16,40,1]{2,1,3,0:T(8,128)S(1)} %collective-permute-done.5) | data formatting | bytes 51200 | tf_op jit(solution)/shard_map/ppermute | solution.py:33
  52.8 3.3 %copy.402 = f32[10,16,40,1]{3,2,1,0:T(8,128)} copy(f32[10,16,40,1]{2,1,3,0:T(8,128)} %collective-permute-done.4) | data formatting | bytes 51200 | tf_op jit(solution)/shard_map/ppermute | solution.py:30
  56.0 8.6 %fusion.4 = (f32[16,40]{1,0:T(8,128)S(1)}, f32[5,16,40,128]{3,2,1,0:T(8,128)}) fusion(f32[5,16,40,128]{3,2,1,0:T(8,128)} %copy-done.17, f32[10,16,40,128]{3,2,1,0:T(8,128)} %copy-done.5, f32[10,16,40,1]{3,2,1,0:T(8,128)} %copy.402, f32[5,16,40,1]{3,2,1,0:T(8,128)} %copy.406, f32[5,16,40,127]{3,2,1,0:T(8,128)} %slice.386, f32[10,16,40,1]{3,2,1,0:T(8,128)} %copy.404), kind=kLoop, calls=%fused_computation.18 | loop fusion | flops 3276160 | bytes 8245760 | tf_op jit(solution)/shard_map/reduce_sum | solution.py:154
  64.7 5.6 %psum.14 = f32[16,40]{1,0:T(8,128)S(1)} all-reduce(f32[16,40]{1,0:T(8,128)S(1)} %negate_divide_fusion), channel_id=1, replica_groups=mesh['su'=8,'sv'=2,'nrm'=2] {'nrm'}, use_global_device_ids=true, to_apply=%region_1.2 | all-reduce | flops 640 | bytes 5120 | tf_op jit(solution)/shard_map/psum | solution.py:163
  70.4 15.0 %all-gather = f32[8,1,40]{2,1,0:T(1,128)S(1)} all-gather(f32[1,1,40]{2,1,0:T(1,128)S(1)} %slice_bitcast_fusion), channel_id=1, replica_groups=mesh['su'=8,'sv'=2,'nrm'=2] {'su'}, dimensions={0}, use_global_device_ids=true | all-gather | bytes 1440 | tf_op jit(solution)/shard_map/all_gather | solution.py:15
  85.7 5.0 %psum.15 = f32[16,40]{1,0:T(8,128)S(1)} all-reduce(f32[16,40]{1,0:T(8,128)S(1)} %add_select_fusion), channel_id=1, replica_groups=mesh['su'=8,'sv'=2,'nrm'=2] {'nrm'}, use_global_device_ids=true, to_apply=%region_7.8 | all-reduce | flops 640 | bytes 5120 | tf_op jit(solution)/shard_map/psum | solution.py:40
  91.0 3.9 %fusion.19 = f32[5,16,40,128]{3,2,1,0:T(8,128)S(1)} fusion(f32[7,20,2,128]{3,2,1,0:T(2,128)} %collective-permute-done.3, f32[7,2,40,128]{3,2,1,0:T(8,128)} %collective-permute-done.1, f32[7,2,40,128]{3,2,1,0:T(8,128)} %collective-permute-done, f32[1,16,40,128]{3,2,1,0:T(8,128)} %copy-done.6, f32[1,16,40,128]{3,2,1,0:T(8,128)} %copy-done.9, ...), kind=kLoop, calls=%fused_computation.43 | loop fusion | flops 10240000 | bytes 4792320 | tf_op jit(solution)/shard_map/div | solution.py:91
  100.0 1.3 %fusion.1 = f32[5,16,44,128]{3,2,1,0:T(8,128)S(1)} fusion(f32[7,20,2,128]{3,2,1,0:T(2,128)} %collective-permute-done.3, f32[7,20,2,128]{3,2,1,0:T(2,128)S(1)} %collective-permute-done.2, f32[7,2,40,128]{3,2,1,0:T(8,128)} %collective-permute-done.1, f32[7,2,40,128]{3,2,1,0:T(8,128)} %collective-permute-done, f32[1,16,40,128]{3,2,1,0:T(8,128)S(1)} %copy-done.8, ...), kind=kLoop, calls=%fused_computation.9 | loop fusion | flops 3153920 | bytes 5316608 | tf_op jit(solution)/shard_map/mul | solution.py:95
  102.5 2.7 %fusion.10 = f32[5,16,40,128]{3,2,1,0:T(8,128)} fusion(f32[5,16,40,128]{3,2,1,0:T(8,128)S(1)} %get-tuple-element.121, f32[5,16,44,128]{3,2,1,0:T(8,128)S(1)} %fusion.1, f32[5,20,40,128]{3,2,1,0:T(8,128)S(1)} %copy-done.2, f32[5,16,40,128]{3,2,1,0:T(8,128)S(1)} %copy-done.22, f32[5,16,40,128]{3,2,1,0:T(8,128)S(1)} %add_dynamic-update-slice_fusion.2, ...), kind=kLoop, calls=%fused_computation.26 | loop fusion | flops 9011200 | bytes 26542080 | tf_op jit(solution)/shard_map/add | solution.py:175
  (131 shorter events, 18.4 us)
Async XLA Ops:
  3.1 8.0 %copy-start.17 = (f32[5,16,40,128]{3,2,1,0:T(8,128)}, f32[5,16,40,128]{3,2,1,0:T(8,128)S(1)}, u32[]{:S(2)}) copy-start(f32[5,16,40,128]{3,2,1,0:T(8,128)S(1)} %get-tuple-element.103) | copy-start | bytes 4915204
  4.9 7.1 %copy-start.3 = (f32[10,16,40,128]{3,2,1,0:T(8,128)}, f32[10,16,40,128]{3,2,1,0:T(8,128)S(1)}, u32[]{:S(2)}) copy-start(f32[10,16,40,128]{3,2,1,0:T(8,128)S(1)} %get-tuple-element.131) | copy-start | bytes 9830404
  5.0 7.1 %copy-start.6 = (f32[1,16,40,128]{3,2,1,0:T(8,128)}, f32[1,16,40,128]{3,2,1,0:T(8,128)S(1)}, u32[]{:S(2)}) copy-start(f32[1,16,40,128]{3,2,1,0:T(8,128)S(1)} %get-tuple-element.127) | copy-start | bytes 983044
  5.0 7.1 %copy-start.9 = (f32[1,16,40,128]{3,2,1,0:T(8,128)}, f32[1,16,40,128]{3,2,1,0:T(8,128)S(1)}, u32[]{:S(2)}) copy-start(f32[1,16,40,128]{3,2,1,0:T(8,128)S(1)} %get-tuple-element.128) | copy-start | bytes 983044
  5.0 7.1 %copy-start.20 = (f32[5,16,40,128]{3,2,1,0:T(8,128)}, f32[5,16,40,128]{3,2,1,0:T(8,128)S(1)}, u32[]{:S(2)}) copy-start(f32[5,16,40,128]{3,2,1,0:T(8,128)S(1)} %get-tuple-element.126) | copy-start | bytes 4915204
  5.0 5.4 %copy-start.27 = (f32[5,16,40]{2,1,0:T(8,128)S(1)}, f32[5,16,40]{2,1,0:T(8,128)}, u32[]{:S(2)}) copy-start(f32[5,16,40]{2,1,0:T(8,128)} %param.14) | copy-start | bytes 38404
  5.8 6.3 %copy-start.30 = (f32[5,16,40]{2,1,0:T(8,128)S(1)}, f32[5,16,40]{2,1,0:T(8,128)}, u32[]{:S(2)}) copy-start(f32[5,16,40]{2,1,0:T(8,128)} %param.15) | copy-start | bytes 38404
  5.8 6.3 %copy-start.31 = (f32[5,16,40]{2,1,0:T(8,128)S(1)}, f32[5,16,40]{2,1,0:T(8,128)}, u32[]{:S(2)}) copy-start(f32[5,16,40]{2,1,0:T(8,128)} %param.16) | copy-start | bytes 38404
  5.8 6.9 %collective-permute-start = (f32[7,2,40,128]{3,2,1,0:T(8,128)}, f32[7,2,40,128]{3,2,1,0:T(8,128)}, u32[]{:S(2)}, u32[]{:S(2)}) collective-permute-start(f32[7,2,40,128]{3,2,1,0:T(8,128)} %get-tuple-element.114), channel_id=1, source_target_pairs={{0,4},{4,8},{8,12},{12,16},{16,20},{20,24},{24,28},{1,5},{5,9},{9,... | collective-permute-start | bytes 860168 | tf_op jit(solution)/shard_map/ppermute | solution.py:30
  9.1 5.3 %collective-permute-start.1 = (f32[7,2,40,128]{3,2,1,0:T(8,128)}, f32[7,2,40,128]{3,2,1,0:T(8,128)}, u32[]{:S(2)}, u32[]{:S(2)}) collective-permute-start(f32[7,2,40,128]{3,2,1,0:T(8,128)} %get-tuple-element.115), channel_id=1, source_target_pairs={{4,0},{8,4},{12,8},{16,12},{20,16},{24,20},{28,24},{5,1},{9,5},{13... | collective-permute-start | bytes 860168 | tf_op jit(solution)/shard_map/ppermute | solution.py:33
  20.8 3.9 %copy-start.5 = (f32[10,16,40,128]{3,2,1,0:T(8,128)}, f32[10,16,40,128]{3,2,1,0:T(8,128)S(1)}, u32[]{:S(2)}) copy-start(f32[10,16,40,128]{3,2,1,0:T(8,128)S(1)} %get-tuple-element.130) | copy-start | bytes 9830404
  28.0 24.8 %collective-permute-start.4 = (f32[10,16,40,1]{2,1,3,0:T(8,128)}, f32[10,16,40,1]{2,1,3,0:T(8,128)}, u32[]{:S(2)}, u32[]{:S(2)}) collective-permute-start(f32[10,16,40,1]{2,1,3,0:T(8,128)} %copy.401), channel_id=1, source_target_pairs={{0,1},{2,3},{4,5},{6,7},{8,9},{10,11},{12,13},{14,15},{16,17},{18,... | collective-permute-start | bytes 76808 | tf_op jit(solution)/shard_map/ppermute | solution.py:30
  35.3 8.0 %copy-start.7 = (f32[1,16,40,128]{3,2,1,0:T(8,128)S(1)}, f32[1,16,40,128]{3,2,1,0:T(8,128)}, u32[]{:S(2)}) copy-start(f32[1,16,40,128]{3,2,1,0:T(8,128)} %copy-done.6) | copy-start | bytes 983044
  35.3 8.0 %copy-start.10 = (f32[1,16,40,128]{3,2,1,0:T(8,128)S(1)}, f32[1,16,40,128]{3,2,1,0:T(8,128)}, u32[]{:S(2)}) copy-start(f32[1,16,40,128]{3,2,1,0:T(8,128)} %copy-done.9) | copy-start | bytes 983044
  35.3 13.2 %collective-permute-start.5 = (f32[10,16,40,1]{2,1,3,0:T(8,128)}, f32[10,16,40,1]{2,1,3,0:T(8,128)S(1)}, u32[]{:S(2)}, u32[]{:S(2)}) collective-permute-start(f32[10,16,40,1]{2,1,3,0:T(8,128)} %copy.403), channel_id=1, source_target_pairs={{1,0},{3,2},{5,4},{7,6},{9,8},{11,10},{13,12},{15,14},{17,16},{19,... | collective-permute-start | bytes 76808 | tf_op jit(solution)/shard_map/ppermute | solution.py:33
  38.6 52.3 %collective-permute-start.2 = (f32[7,20,2,128]{3,2,1,0:T(2,128)}, f32[7,20,2,128]{3,2,1,0:T(2,128)S(1)}, u32[]{:S(2)}, u32[]{:S(2)}) collective-permute-start(f32[7,20,2,128]{3,2,1,0:T(2,128)} %get-tuple-element.108), channel_id=1, source_target_pairs={{0,2},{1,3},{4,6},{5,7},{8,10},{9,11},{12,14},{13,15},{16,18},{17,... | collective-permute-start | bytes 430088 | tf_op jit(solution)/shard_map/ppermute | solution.py:30
  42.0 48.9 %collective-permute-start.3 = (f32[7,20,2,128]{3,2,1,0:T(2,128)}, f32[7,20,2,128]{3,2,1,0:T(2,128)}, u32[]{:S(2)}, u32[]{:S(2)}) collective-permute-start(f32[7,20,2,128]{3,2,1,0:T(2,128)} %get-tuple-element.109), channel_id=1, source_target_pairs={{2,0},{3,1},{6,4},{7,5},{10,8},{11,9},{14,12},{15,13},{18,16},{19,... | collective-permute-start | bytes 430088 | tf_op jit(solution)/shard_map/ppermute | solution.py:33
  56.0 8.7 %copy-start.32 = (f32[16,40]{1,0:T(8,128)S(1)}, f32[16,40]{1,0:T(8,128)}, u32[]{:S(2)}) copy-start(f32[16,40]{1,0:T(8,128)} %param.13) | copy-start | bytes 7684
  56.0 14.3 %copy-start.33 = (f32[16,40]{1,0:T(8,128)S(1)}, f32[16,40]{1,0:T(8,128)}, u32[]{:S(2)}) copy-start(f32[16,40]{1,0:T(8,128)} %get-tuple-element.70) | copy-start | bytes 7684
  56.0 14.3 %copy-start.34 = (s32[16,40]{1,0:T(8,128)S(1)}, s32[16,40]{1,0:T(8,128)}, u32[]{:S(2)}) copy-start(s32[16,40]{1,0:T(8,128)} %param.17) | copy-start | bytes 7684
  90.8 4.1 %copy-start.35 = (f32[16,40]{1,0:T(8,128)}, f32[16,40]{1,0:T(8,128)S(1)}, u32[]{:S(2)}) copy-start(f32[16,40]{1,0:T(8,128)S(1)} %psum.15) | copy-start | bytes 7684
  90.9 4.0 %copy-start.12 = (f32[5,16,40,128]{3,2,1,0:T(8,128)S(1)}, f32[5,16,40,128]{3,2,1,0:T(8,128)}, u32[]{:S(2)}) copy-start(f32[5,16,40,128]{3,2,1,0:T(8,128)} %get-tuple-element.105) | copy-start | bytes 4915204
  90.9 4.0 %copy-start.19 = (f32[1,16,40,128]{3,2,1,0:T(8,128)S(1)}, f32[1,16,40,128]{3,2,1,0:T(8,128)}, u32[]{:S(2)}) copy-start(f32[1,16,40,128]{3,2,1,0:T(8,128)} %copy-done.18) | copy-start | bytes 983044
  90.9 4.0 %copy-start.26 = (f32[1,16,40,128]{3,2,1,0:T(8,128)S(1)}, f32[1,16,40,128]{3,2,1,0:T(8,128)}, u32[]{:S(2)}) copy-start(f32[1,16,40,128]{3,2,1,0:T(8,128)} %get-tuple-element.125) | copy-start | bytes 983044
  (18 other events, 34.1 us)
where the time goes:
time: 107 us; the launch traced here: 105 us
  other arithmetic  32.9 us (31%)
  local copies, waits for them, and re-layouts  29 us (27%)
  blocking collectives  25.7 us (24%)
  starting transfers between devices  14.7 us (14%)
  waiting for transfers between devices  1.56 us (1%)
  between operations  1.27 us (1%)
    all_gather x1, blocking collectives, prefix(): gathered = lax.all_gather(part, axis)  15 us
    ppermute x3, starting transfers between devices, extended(): lax.ppermute(lax.slice_in_dim(block, block.shape[dim] - width, None, axis...  10.7 us
    reduce_sum x1, other arithmetic, local(): jnp.sum(scaled * (flux_above - flux_below), axis=(0, 3))  8.65 us
    unnamed x73, local copies, waits for them, and re-layouts  8.41 us
    slice x2, local copies, waits for them, and re-layouts, extended(): lax.slice_in_dim(block, block.shape[dim] - width, None, axis=dim)  7.2 us
    psum x1, blocking collectives, local(): metric = lax.psum(metric_part, 'nrm')  5.62 us
    mul x4, other arithmetic, tangent_parts(): weighted = padded_radius[None] * padded_adjoint  5.57 us
    psum x1, blocking collectives, spread(): return lax.psum(block, axis)  5.02 us
  transfers between devices with their start and end apart: 6, of which 1 were waited for; matrix products, arithmetic and copies ran while one was open for 27% of the time, Pallas kernels for 0%

commit v1 on v0

v1 whole, which is shorter than its diff:
```python
import functools
import math

import jax
import jax.numpy as jnp
from jax import lax
from jax.experimental import pallas as pl
from jax.experimental.pallas import tpu as pltpu
from jax.sharding import PartitionSpec as P

gamma_ratio = 1.4
gamma_less = gamma_ratio - 1.0
damping_coef = 0.0625
stretch_rate = 2.2
MESH = pl.DeviceIdType.MESH
SUB = 8
LANES = 128


def thermo(state):
    speed_square = state[1] * state[1] + state[2] * state[2] + state[3] * state[3]
    kinetic = 0.5 * gamma_less * speed_square
    enthalpy = gamma_ratio * state[4] / (gamma_less * state[0]) + 0.5 * speed_square
    return (kinetic, enthalpy)


def line_flux(state, enthalpy):
    mass_flow = state[0] * state[3]
    return [
        mass_flow,
        mass_flow * state[1],
        mass_flow * state[2],
        mass_flow * state[3] + state[4],
        mass_flow * enthalpy,
    ]


def flux_transpose_normal(state, kinetic, enthalpy, adjoint):
    normal_speed = state[3]
    projected = adjoint[3]
    dotted = state[1] * adjoint[1] + state[2] * adjoint[2] + state[3] * adjoint[3]
    energy_term = adjoint[4]
    mass_row = (
        kinetic * projected
        - normal_speed * dotted
        + normal_speed * (kinetic - enthalpy) * energy_term
    )
    common = adjoint[0] + dotted + enthalpy * energy_term
    shared = projected + normal_speed * energy_term
    pieces = [mass_row]
    for component in (1, 2, 3):
        entry = normal_speed * adjoint[component] - gamma_less * state[component] * shared
        if component == 3:
            entry = entry + common
        pieces.append(entry)
    pieces.append(gamma_less * projected + gamma_ratio * normal_speed * energy_term)
    return pieces


def kernel(
    n_su, n_sv,
    height_ref, shock_ref, by_height_ref, by_slope_ref, fitted_ref,
    prim_hbm, psi_hbm, obj_hbm,
    out_hbm, slope_ref,
    psi, prim, out, normal, enth, rad_u, rad_v,
    sv_send, sv_recv, edge_send, edge_recv, top_pack, turn, height_t, slope_t,
    half_send, half_recv, tot_send, tot_recv,
    load_sem, store_sem, send_sem, recv_sem, tot_ssem, tot_rsem,
):
    rows, cols = prim.shape[1], prim.shape[2]
    chunks = cols // SUB
    su, sv, nrm = lax.axis_index("su"), lax.axis_index("sv"), lax.axis_index("nrm")
    own = pl.ds(SUB, cols)

    load_psi = pltpu.make_async_copy(psi_hbm, psi.at[:, pl.ds(2, rows), own], load_sem.at[0])
    load_prim = pltpu.make_async_copy(prim_hbm, prim, load_sem.at[1])
    load_obj = pltpu.make_async_copy(obj_hbm, out, load_sem.at[2])
    load_psi.start()
    load_prim.start()
    load_obj.start()

    barrier = pltpu.get_barrier_semaphore()
    for step in range(1, n_su):
        pl.semaphore_signal(
            barrier, inc=1, device_id={"su": lax.rem(su + step, n_su)}, device_id_type=MESH
        )
    pl.semaphore_signal(barrier, inc=1, device_id={"nrm": 1 - nrm}, device_id_type=MESH)

    @pl.when(sv > 0)
    def _():
        pl.semaphore_signal(barrier, inc=1, device_id={"sv": sv - 1}, device_id_type=MESH)

    @pl.when(sv < n_sv - 1)
    def _():
        pl.semaphore_signal(barrier, inc=1, device_id={"sv": sv + 1}, device_id_type=MESH)

    def remote(src, dst, slot, where):
        return pltpu.make_async_remote_copy(
            src_ref=src,
            dst_ref=dst,
            send_sem=send_sem.at[slot],
            recv_sem=recv_sem.at[slot],
            device_id=where,
            device_id_type=MESH,
        )

    psi_down = remote(
        psi_hbm.at[:, pl.ds(0, 2)], psi.at[:, pl.ds(rows + 2, 2), own], 0, {"su": su - 1}
    )
    psi_up = remote(
        psi_hbm.at[:, pl.ds(rows - 2, 2)], psi.at[:, pl.ds(0, 2), own], 1, {"su": su + 1}
    )
    rad_down = remote(rad_u.at[pl.ds(2, 2)], rad_u.at[pl.ds(rows + 2, 2)], 2, {"su": su - 1})
    rad_up = remote(rad_u.at[pl.ds(rows, 2)], rad_u.at[pl.ds(0, 2)], 3, {"su": su + 1})
    sv_down = remote(sv_send.at[0], sv_recv.at[1], 4, {"sv": sv - 1})
    sv_up = remote(sv_send.at[1], sv_recv.at[0], 5, {"sv": sv + 1})
    edge = remote(edge_send, edge_recv, 6, {"nrm": 1 - nrm})
    half = remote(half_send, half_recv, 7, {"nrm": 1 - nrm})

    lane = lax.broadcasted_iota(jnp.int32, (1, LANES), 1)
    total_depth = 2 * LANES
    place = (nrm * LANES + lane).astype(jnp.float32)
    fraction = (place + 0.5) / total_depth

    def half_inverse(position):
        return 0.5 * jnp.exp(stretch_rate * (1.0 - (position + 0.5) / total_depth))

    below = jnp.where(lane == 0, 0.0, half_inverse(place - 1.0))
    above = jnp.where(lane == LANES - 1, 0.0, half_inverse(place + 1.0))
    target = jnp.where(nrm == 0, LANES - 1, 0)
    edge_weight = jnp.where(
        lane == target,
        jnp.where(nrm == 0, -half_inverse(place + 1.0), half_inverse(place - 1.0)),
        0.0,
    )

    turn[...] = jnp.zeros_like(turn)
    turn[0:rows, 0:cols] = 1.0 / height_ref[...]
    height_t[...] = turn[...].T[0:cols]

    @pl.when(su == 0)
    def _():
        psi[:, 0:2, SUB : SUB + cols] = jnp.zeros((5, 2, cols, LANES), jnp.float32)
        rad_u[0:2] = jnp.zeros((2, cols, LANES), jnp.float32)

    @pl.when(su == n_su - 1)
    def _():
        psi[:, rows + 2 : rows + 4, SUB : SUB + cols] = jnp.zeros((5, 2, cols, LANES), jnp.float32)
        rad_u[rows + 2 : rows + 4] = jnp.zeros((2, cols, LANES), jnp.float32)

    @pl.when(sv == 0)
    def _():
        sv_recv[0] = jnp.zeros((6, rows, 2, LANES), jnp.float32)

    @pl.when(sv == n_sv - 1)
    def _():
        sv_recv[1] = jnp.zeros((6, rows, 2, LANES), jnp.float32)

    neighbours = n_su + (sv > 0).astype(jnp.int32) + (sv < n_sv - 1).astype(jnp.int32)
    pl.semaphore_wait(barrier, neighbours)

    @pl.when(su > 0)
    def _():
        psi_down.start()

    @pl.when(su < n_su - 1)
    def _():
        psi_up.start()

    load_psi.wait()

    def pack(row, carry):
        top, bottom = carry
        for comp in range(5):
            spot = comp * rows + row
            rolled = pltpu.roll(psi[comp, row + 2, SUB : SUB + cols, :], spot + 1, 1)
            top = jnp.where(lane == spot, rolled, top)
            bottom = jnp.where(lane == spot + 1, rolled, bottom)
        return (top, bottom)

    blank = jnp.zeros((cols, LANES), jnp.float32)
    top, bottom = lax.fori_loop(0, rows, pack, (blank, blank))
    top_pack[...] = top
    edge_send[...] = jnp.where(nrm == 0, top, pltpu.roll(bottom, LANES - 1, 1))
    edge.start()

    load_prim.wait()

    def radii(row, carry):
        for chunk in range(chunks):
            part = slice(chunk * SUB, chunk * SUB + SUB)
            state = [prim[comp, row, part, :] for comp in range(5)]
            square = gamma_ratio * state[4] / state[0]
            sound = jnp.sqrt(square)
            speed_square = state[1] * state[1] + state[2] * state[2] + state[3] * state[3]
            enth[row, part, :] = square * (1.0 / gamma_less) + 0.5 * speed_square
            rad_u[row + 2, part, :] = damping_coef * (jnp.abs(state[1]) + sound)
            rad_v[row, SUB + chunk * SUB : 2 * SUB + chunk * SUB, :] = damping_coef * (
                jnp.abs(state[2]) + sound
            )
        for comp in range(5):
            sv_send[0, comp, row] = psi[comp, row + 2, SUB : SUB + 2, :]
            sv_send[1, comp, row] = psi[comp, row + 2, SUB + cols - 2 : SUB + cols, :]
        sv_send[0, 5, row] = rad_v[row, SUB : SUB + 2, :]
        sv_send[1, 5, row] = rad_v[row, SUB + cols - 2 : SUB + cols, :]
        return carry

    lax.fori_loop(0, rows, radii, 0)

    @pl.when(sv > 0)
    def _():
        sv_down.start()

    @pl.when(sv < n_sv - 1)
    def _():
        sv_up.start()

    @pl.when(su > 0)
    def _():
        rad_down.start()

    @pl.when(su < n_su - 1)
    def _():
        rad_up.start()

    edge.wait_recv()

    def metric_row(row, sums):
        scale = pltpu.roll(height_t[...], LANES - row, 1)[:, 0:1]
        pieces = []
        for chunk in range(chunks):
            part = slice(chunk * SUB, chunk * SUB + SUB)
            state = [prim[comp, row, part, :] for comp in range(5)]
            flux = line_flux(state, enth[row, part, :])
            factor = jnp.broadcast_to(scale[part], (SUB, LANES))
            total = None
            for comp in range(5):
                value = psi[comp, row + 2, SUB + chunk * SUB : 2 * SUB + chunk * SUB, :]
                shift = lax.rem(target - (comp * rows + row) + LANES, LANES)
                difference = (
                    pltpu.roll(value, 1, 1) * below
                    - pltpu.roll(value, LANES - 1, 1) * above
                    + pltpu.roll(edge_recv[part, :], shift, 1) * edge_weight
                ) * factor
                normal[comp, row, part, :] = difference
                term = flux[comp] * difference
                total = term if total is None else total + term
            pieces.append(jnp.sum(total, axis=1, keepdims=True))
        return jnp.where(lane == row, jnp.concatenate(pieces, 0), sums)

    sums = lax.fori_loop(0, rows, metric_row, blank)

    turn[...] = jnp.zeros_like(turn)
    turn[0:cols, :] = sums
    line_sums = turn[...].T[0:rows, 0:cols]
    turn[0:cols, :] = top_pack[...]
    tops = turn[...].T
    inverse = 1.0 / height_ref[...]
    last = 0.5 * math.exp(stretch_rate * 0.5 / total_depth)
    top_scaled = [
        tops[comp * rows : comp * rows + rows, 0:cols] * (last * inverse) for comp in range(5)
    ]
    shock = [shock_ref[comp] for comp in range(5)]
    shock_kinetic, shock_enthalpy = thermo(shock)
    shock_flux = line_flux(shock, shock_enthalpy)
    shock_adjoint = flux_transpose_normal(shock, shock_kinetic, shock_enthalpy, top_scaled)
    fitted = fitted_ref[...].astype(jnp.float32)
    front_flux = sum(top_scaled[comp] * shock_flux[comp] for comp in range(5))
    front_height = fitted * sum(shock_adjoint[comp] * by_height_ref[comp] for comp in range(5))
    front_slope = fitted * sum(shock_adjoint[comp] * by_slope_ref[comp] for comp in range(5))
    on_front = nrm == 1
    half_send[...] = jnp.zeros_like(half_send)
    half_send[0, :, 0:cols] = (
        jnp.where(on_front, front_height - front_flux * inverse, 0.0) - line_sums * inverse
    )
    half_send[1, :, 0:cols] = jnp.where(on_front, front_slope, 0.0)
    half.start()

    @pl.when(sv > 0)
    def _():
        sv_up.wait_recv()

    @pl.when(sv < n_sv - 1)
    def _():
        sv_down.wait_recv()

    def unpack(row, carry):
        for comp in range(5):
            psi[comp, row + 2, SUB - 2 : SUB, :] = sv_recv[0, comp, row]
            psi[comp, row + 2, SUB + cols : SUB + cols + 2, :] = sv_recv[1, comp, row]
        rad_v[row, SUB - 2 : SUB, :] = sv_recv[0, 5, row]
        rad_v[row, SUB + cols : SUB + cols + 2, :] = sv_recv[1, 5, row]
        return carry

    lax.fori_loop(0, rows, unpack, 0)
    load_obj.wait()

    def residual_row(row, carry):
        for chunk in range(chunks):
            first = chunk * SUB
            part = slice(first, first + SUB)
            wide = slice(SUB + first, 2 * SUB + first)
            density, u1, u2, u3, pressure = [prim[comp, row, part, :] for comp in range(5)]
            enthalpy = enth[row, part, :]
            ru = [rad_u[row + offset, part, :] for offset in range(5)]
            rv = [rad_v[row, wide.start + offset - 2 : wide.stop + offset - 2, :] for offset in range(5)]
            ruv = 6.0 * (ru[2] + rv[2])
            g1, g2, damped = [], [], []
            for comp in range(5):
                centre = psi[comp, row + 2, wide, :]
                along = [psi[comp, row + offset, wide, :] for offset in (0, 1, 3, 4)]
                across = [
                    psi[comp, row + 2, wide.start + offset : wide.stop + offset, :]
                    for offset in (-2, -1, 1, 2)
                ]
                g1.append((along[1] - along[2]) * (2.0 / 3.0) - (along[0] - along[3]) * (1.0 / 12.0))
                g2.append((across[1] - across[2]) * (2.0 / 3.0) - (across[0] - across[3]) * (1.0 / 12.0))
                far = ru[0] * along[0] + ru[4] * along[3] + rv[0] * across[0] + rv[4] * across[3]
                near = ru[1] * along[1] + ru[3] * along[2] + rv[1] * across[1] + rv[3] * across[2]
                damped.append(far - 4.0 * near + ruv * centre)
            g3 = [normal[comp, row, part, :] for comp in range(5)]
            kinetic = (0.5 * gamma_less) * (u1 * u1 + u2 * u2 + u3 * u3)
            speeds = (u1, u2, u3)
            grads = (g1, g2, g3)
            spread = g1[1] + g2[2] + g3[3]
            energy = u1 * g1[4] + u2 * g2[4] + u3 * g3[4]
            carried = [u1 * g1[b] + u2 * g2[b] + u3 * g3[b] for b in (1, 2, 3)]
            shared = gamma_less * (spread + energy)
            out[0, row, part, :] = (
                out[0, row, part, :]
                + damped[0]
                + kinetic * spread
                - (u1 * carried[0] + u2 * carried[1] + u3 * carried[2])
                + (kinetic - enthalpy) * energy
            )
            for b in (1, 2, 3):
                g = grads[b - 1]
                dotted = u1 * g[1] + u2 * g[2] + u3 * g[3]
                out[b, row, part, :] = (
                    out[b, row, part, :]
                    + damped[b]
                    + carried[b - 1]
                    - speeds[b - 1] * shared
                    + (g[0] + dotted + enthalpy * g[4])
                )
            out[4, row, part, :] = (
                out[4, row, part, :] + damped[4] + gamma_less * spread + gamma_ratio * energy
            )
        return carry

    middle = rows // 2
    lax.fori_loop(2, middle, residual_row, 0)

    half.wait_recv()
    summed = half_send[0, :, 0:cols] + half_recv[0, :, 0:cols]
    front_slope = half_send[1, :, 0:cols] + half_recv[1, :, 0:cols]
    step = 1
    while step < rows:
        summed = summed + jnp.concatenate(
            [summed[step:], jnp.zeros((step, cols), jnp.float32)], 0
        )
        step *= 2
    tot_send[...] = jnp.zeros_like(tot_send)
    tot_send[:, 0:cols] = summed[0:1]

    def total_copy(source, dest):
        return pltpu.make_async_remote_copy(
            src_ref=tot_send,
            dst_ref=tot_recv.at[source],
            send_sem=tot_ssem.at[dest],
            recv_sem=tot_rsem.at[source],
            device_id={"su": dest},
            device_id_type=MESH,
        )

    for other in range(n_su - 1):
        @pl.when(other < su)
        def _(other=other):
            total_copy(su, other).start()

    lax.fori_loop(middle, rows - 2, residual_row, 0)

    @pl.when(su > 0)
    def _():
        psi_up.wait_recv()
        rad_up.wait_recv()

    @pl.when(su < n_su - 1)
    def _():
        psi_down.wait_recv()
        rad_down.wait_recv()

    lax.fori_loop(0, 2, residual_row, 0)
    lax.fori_loop(rows - 2, rows, residual_row, 0)

    for other in range(1, n_su):
        @pl.when(other > su)
        def _(other=other):
            total_copy(other, su).wait_recv()

    upstream = jnp.zeros((1, cols), jnp.float32)
    for other in range(n_su - 1, 0, -1):
        upstream = upstream + jnp.where(other > su, tot_recv[other, :, 0:cols], 0.0)
    slope = (summed + upstream) * (1.0 / (rows * n_su)) + front_slope
    slope_ref[...] = slope
    turn[...] = jnp.zeros_like(turn)
    turn[0:rows, 0:cols] = slope
    slope_t[...] = turn[...].T[0:cols]

    def store(row):
        return pltpu.make_async_copy(
            out.at[:, pl.ds(row, 1)], out_hbm.at[:, pl.ds(row, 1)], store_sem.at[row]
        )

    def slope_row(row, carry):
        column = pltpu.roll(slope_t[...], LANES - row, 1)[:, 0:1]
        for chunk in range(chunks):
            part = slice(chunk * SUB, chunk * SUB + SUB)
            state = [prim[comp, row, part, :] for comp in range(5)]
            flux = line_flux(state, enth[row, part, :])
            weight = jnp.broadcast_to(column[part], (SUB, LANES)) * fraction
            for comp in range(5):
                out[comp, row, part, :] = out[comp, row, part, :] + weight * flux[comp]
        store(row).start()
        return carry

    lax.fori_loop(0, rows, slope_row, 0)

    @pl.when(su > 0)
    def _():
        psi_down.wait_send()
        rad_down.wait_send()

    @pl.when(su < n_su - 1)
    def _():
        psi_up.wait_send()
        rad_up.wait_send()

    @pl.when(sv > 0)
    def _():
        sv_down.wait_send()

    @pl.when(sv < n_sv - 1)
    def _():
        sv_up.wait_send()

    edge.wait_send()
    half.wait_send()
    for other in range(n_su - 1):
        @pl.when(other < su)
        def _(other=other):
            total_copy(su, other).wait_send()

    def finish(row, carry):
        store(row).wait()
        return carry

    lax.fori_loop(0, rows, finish, 0)


def local(
    n_su, n_sv,
    primitive, adjoint_state, objective_grad, front_height,
    shock_state, state_by_height, state_by_slope, fitted_flags,
):
    _, rows, cols, depth = primitive.shape
    f32 = jnp.float32
    vmem = pl.BlockSpec(memory_space=pltpu.VMEM)
    hbm = pl.BlockSpec(memory_space=pl.ANY)
    block = (5, rows, cols, depth)
    wide = cols + 2 * SUB
    dma = pltpu.SemaphoreType.DMA
    return pl.pallas_call(
        functools.partial(kernel, n_su, n_sv),
        out_shape=(
            jax.ShapeDtypeStruct(block, f32),
            jax.ShapeDtypeStruct((rows, cols), f32),
        ),
        in_specs=[vmem] * 5 + [hbm] * 3,
        out_specs=(hbm, vmem),
        scratch_shapes=[
            pltpu.VMEM((5, rows + 4, wide, depth), f32),
            pltpu.VMEM(block, f32),
            pltpu.VMEM(block, f32),
            pltpu.VMEM(block, f32),
            pltpu.VMEM((rows, cols, depth), f32),
            pltpu.VMEM((rows + 4, cols, depth), f32),
            pltpu.VMEM((rows, wide, depth), f32),
            pltpu.VMEM((2, 6, rows, 2, depth), f32),
            pltpu.VMEM((2, 6, rows, 2, depth), f32),
            pltpu.VMEM((cols, LANES), f32),
            pltpu.VMEM((cols, LANES), f32),
            pltpu.VMEM((cols, LANES), f32),
            pltpu.VMEM((LANES, LANES), f32),
            pltpu.VMEM((cols, LANES), f32),
            pltpu.VMEM((cols, LANES), f32),
            pltpu.VMEM((2, rows, LANES), f32),
            pltpu.VMEM((2, rows, LANES), f32),
            pltpu.VMEM((1, LANES), f32),
            pltpu.VMEM((n_su, 1, LANES), f32),
            dma((3,)),
            dma((rows,)),
            dma((8,)),
            dma((8,)),
            dma((n_su,)),
            dma((n_su,)),
        ],
        compiler_params=pltpu.CompilerParams(
            collective_id=0, has_side_effects=True, vmem_limit_bytes=40 * 1024 * 1024
        ),
    )(
        front_height, shock_state, state_by_height, state_by_slope, fitted_flags,
        primitive, adjoint_state, objective_grad,
    )


def solution(mesh):
    assert mesh.shape["nrm"] == 2
    surface = P(None, "su", "sv")
    volume = P(None, "su", "sv", "nrm")
    return jax.shard_map(
        functools.partial(local, mesh.shape["su"], mesh.shape["sv"]),
        mesh=mesh,
        in_specs=(volume,) * 3 + (P("su", "sv"),) + (surface,) * 3 + (P("su", "sv"),),
        out_specs=(volume, P("su", "sv")),
        check_vma=False,
    )
```

time: 107 us -> 35.3 us (0.33); the launches traced: 105 us -> 34.9 us
  other arithmetic: 32.9 us -> 0 us
  blocking collectives: 25.7 us -> 0 us
  Pallas kernels: 0 us -> 24.4 us
  local copies, waits for them, and re-layouts: 29 us -> 9.77 us
  starting transfers between devices: 14.7 us -> 0 us
  waiting for transfers between devices: 1.56 us -> 0 us
    pallas_call x0 -> x1, Pallas kernels: none -> 24.4 us  [local(): pl.pallas_call(functools.partial(kernel, n_su, n_sv), out_shape=(jax.Shap...]
    all_gather x1 -> x0, blocking collectives: 15 us -> none  [prefix(): gathered = lax.all_gather(part, axis)]
    ppermute x6 -> x0, starting transfers between devices: 14.7 us -> none  [the longest x3 10.7 us: extended(): lax.ppermute(lax.slice_in_dim(block, block.shape[dim] - width, None, axis...]
    slice x5 -> x0, local copies, waits for them, and re-layouts: 13.1 us -> none  [the longest x2 7.2 us: extended(): lax.slice_in_dim(block, block.shape[dim] - width, None, axis=dim)]
    psum x2 -> x0, blocking collectives: 10.6 us -> none  [the longest x1 5.62 us: local(): metric = lax.psum(metric_part, 'nrm')]
    reduce_sum x2 -> x0, other arithmetic: 9.26 us -> none  [the longest x1 8.65 us: local(): jnp.sum(scaled * (flux_above - flux_below), axis=(0, 3))]
    mul x7 -> x0, other arithmetic: 6.68 us -> none  [the longest x4 5.57 us: tangent_parts(): weighted = padded_radius[None] * padded_adjoint]
    ppermute x2 -> x0, local copies, waits for them, and re-layouts: 5.72 us -> none  [the longest x1 3.26 us: extended(): lax.ppermute(lax.slice_in_dim(block, block.shape[dim] - width, None, axis...]
  transfers between devices with their start and end apart: 6 -> 0, of which waited for: 1 -> 0; matrix products, arithmetic and copies ran while one was open for 27% -> 0% of each run, Pallas kernels for 0% -> 0%
where the time goes in v1:
time: 35.3 us; the launch traced here: 34.9 us
  Pallas kernels  24.4 us (69%)
  local copies, waits for them, and re-layouts  9.77 us (28%)
  between operations  0.66 us (2%)
    pallas_call x1, Pallas kernels, local(): pl.pallas_call(functools.partial(kernel, n_su, n_sv), out_shape=(jax.Shap...  24.4 us
    unnamed x18, local copies, waits for them, and re-layouts  9.77 us

profile of v1, /device:TPU:0, one launch (start us, length us, event | category | flops | bytes accessed | tf_op | source)
XLA Modules:
  0.0 34.9 jit_solution(10158442508678227841)
XLA Ops:
  0.6 0.0 copy-start
  0.6 1.4 %copy-done = f32[5,16,40,128]{3,2,1,0:T(8,128)S(1)} copy-done((f32[5,16,40,128]{3,2,1,0:T(8,128)S(1)}, f32[5,16,40,128]{3,2,1,0:T(8,128)}, u32[]{:S(2)}) %copy-start) | copy-done | bytes 1638424
  2.1 0.0 copy-start.1
  2.1 1.4 %copy-done.1 = f32[5,16,40,128]{3,2,1,0:T(8,128)S(1)} copy-done((f32[5,16,40,128]{3,2,1,0:T(8,128)S(1)}, f32[5,16,40,128]{3,2,1,0:T(8,128)}, u32[]{:S(2)}) %copy-start.1) | copy-done | bytes 1638424
  3.5 0.0 copy-start.2
  3.5 1.4 %copy-done.2 = f32[5,16,40,128]{3,2,1,0:T(8,128)S(1)} copy-done((f32[5,16,40,128]{3,2,1,0:T(8,128)S(1)}, f32[5,16,40,128]{3,2,1,0:T(8,128)}, u32[]{:S(2)}) %copy-start.2) | copy-done | bytes 1638424
  4.9 0.0 copy-start.3
  4.9 0.8 %copy-done.3 = f32[5,16,40]{2,1,0:T(8,128)S(1)} copy-done((f32[5,16,40]{2,1,0:T(8,128)S(1)}, f32[5,16,40]{2,1,0:T(8,128)}, u32[]{:S(2)}) %copy-start.3) | copy-done | bytes 12824
  5.7 0.0 copy-start.4
  5.7 0.8 %copy-done.4 = f32[5,16,40]{2,1,0:T(8,128)S(1)} copy-done((f32[5,16,40]{2,1,0:T(8,128)S(1)}, f32[5,16,40]{2,1,0:T(8,128)}, u32[]{:S(2)}) %copy-start.4) | copy-done | bytes 12824
  6.5 0.0 copy-start.5
  6.5 0.8 %copy-done.5 = f32[5,16,40]{2,1,0:T(8,128)S(1)} copy-done((f32[5,16,40]{2,1,0:T(8,128)S(1)}, f32[5,16,40]{2,1,0:T(8,128)}, u32[]{:S(2)}) %copy-start.5) | copy-done | bytes 12824
  7.3 0.0 copy-start.6
  7.3 0.7 %copy-done.6 = f32[16,40]{1,0:T(8,128)S(1)} copy-done((f32[16,40]{1,0:T(8,128)S(1)}, f32[16,40]{1,0:T(8,128)}, u32[]{:S(2)}) %copy-start.6) | copy-done | bytes 2584
  8.0 0.0 copy-start.7
  8.0 0.7 %copy-done.7 = s32[16,40]{1,0:T(8,128)S(1)} copy-done((s32[16,40]{1,0:T(8,128)S(1)}, s32[16,40]{1,0:T(8,128)}, u32[]{:S(2)}) %copy-start.7) | copy-done | bytes 2584
  8.7 24.4 %shard_map.95 = (f32[5,16,40,128]{3,2,1,0:T(8,128)S(1)}, f32[16,40]{1,0:T(8,128)S(1)}) custom-call(f32[16,40]{1,0:T(8,128)S(1)} %copy-done.6, f32[5,16,40]{2,1,0:T(8,128)S(1)} %copy-done.3, f32[5,16,40]{2,1,0:T(8,128)S(1)} %copy-done.4, f32[5,16,40]{2,1,0:T(8,128)S(1)} %copy-done.5, s32[16,40]{1,0:T(8,128)S(1)} %copy-done.7, f32[5,16,40,128]{3,2,1,0:T(8,128)S(1)} %copy-done, ...), custom_call_target="tpu_custom_call" | custom-call | tf_op jit(solution)/shard_map/pallas_call | solution.py:473
  33.1 1.2 %copy.12 = f32[5,16,40,128]{3,2,1,0:T(8,128)} copy(f32[5,16,40,128]{3,2,1,0:T(8,128)S(1)} %get-tuple-element.4) | data formatting | bytes 3276800
  34.3 0.6 %copy.13 = f32[16,40]{1,0:T(8,128)} copy(f32[16,40]{1,0:T(8,128)S(1)} %get-tuple-element.5) | data formatting | bytes 5120
Async XLA Ops:
  0.6 1.4 %copy-start = (f32[5,16,40,128]{3,2,1,0:T(8,128)S(1)}, f32[5,16,40,128]{3,2,1,0:T(8,128)}, u32[]{:S(2)}) copy-start(f32[5,16,40,128]{3,2,1,0:T(8,128)} %prim_hbm.1) | copy-start | bytes 4915204
  2.1 1.4 %copy-start.1 = (f32[5,16,40,128]{3,2,1,0:T(8,128)S(1)}, f32[5,16,40,128]{3,2,1,0:T(8,128)}, u32[]{:S(2)}) copy-start(f32[5,16,40,128]{3,2,1,0:T(8,128)} %psi_hbm.1) | copy-start | bytes 4915204
  3.5 1.4 %copy-start.2 = (f32[5,16,40,128]{3,2,1,0:T(8,128)S(1)}, f32[5,16,40,128]{3,2,1,0:T(8,128)}, u32[]{:S(2)}) copy-start(f32[5,16,40,128]{3,2,1,0:T(8,128)} %obj_hbm.1) | copy-start | bytes 4915204
  4.9 0.8 %copy-start.3 = (f32[5,16,40]{2,1,0:T(8,128)S(1)}, f32[5,16,40]{2,1,0:T(8,128)}, u32[]{:S(2)}) copy-start(f32[5,16,40]{2,1,0:T(8,128)} %shock_ref.1) | copy-start | bytes 38404
  5.7 0.8 %copy-start.4 = (f32[5,16,40]{2,1,0:T(8,128)S(1)}, f32[5,16,40]{2,1,0:T(8,128)}, u32[]{:S(2)}) copy-start(f32[5,16,40]{2,1,0:T(8,128)} %by_height_ref.1) | copy-start | bytes 38404
  6.5 0.8 %copy-start.5 = (f32[5,16,40]{2,1,0:T(8,128)S(1)}, f32[5,16,40]{2,1,0:T(8,128)}, u32[]{:S(2)}) copy-start(f32[5,16,40]{2,1,0:T(8,128)} %by_slope_ref.1) | copy-start | bytes 38404
  7.3 0.7 %copy-start.6 = (f32[16,40]{1,0:T(8,128)S(1)}, f32[16,40]{1,0:T(8,128)}, u32[]{:S(2)}) copy-start(f32[16,40]{1,0:T(8,128)} %height_ref.1) | copy-start | bytes 7684
  8.0 0.7 %copy-start.7 = (s32[16,40]{1,0:T(8,128)S(1)}, s32[16,40]{1,0:T(8,128)}, u32[]{:S(2)}) copy-start(s32[16,40]{1,0:T(8,128)} %fitted_ref.1) | copy-start | bytes 7684

commit v2 on v1

--- a/solution.py
+++ b/solution.py
@@ -59,13 +59,14 @@
 
 def kernel(
     n_su, n_sv,
+    height_hbm, shock_hbm, by_height_hbm, by_slope_hbm, fitted_hbm,
+    prim_hbm, psi_hbm, obj_hbm,
+    out, prim, enth, slope_ref, slope_t,
+    psi, normal, rad_u, rad_v,
     height_ref, shock_ref, by_height_ref, by_slope_ref, fitted_ref,
-    prim_hbm, psi_hbm, obj_hbm,
-    out_hbm, slope_ref,
-    psi, prim, out, normal, enth, rad_u, rad_v,
-    sv_send, sv_recv, edge_send, edge_recv, top_pack, turn, height_t, slope_t,
+    sv_send, sv_recv, edge_send, edge_recv, top_pack, turn, height_t, height_wide,
     half_send, half_recv, tot_send, tot_recv,
-    load_sem, store_sem, send_sem, recv_sem, tot_ssem, tot_rsem,
+    load_sem, send_sem, recv_sem, tot_ssem, tot_rsem,
 ):
     rows, cols = prim.shape[1], prim.shape[2]
     chunks = cols // SUB
@@ -75,9 +76,16 @@
     load_psi = pltpu.make_async_copy(psi_hbm, psi.at[:, pl.ds(2, rows), own], load_sem.at[0])
     load_prim = pltpu.make_async_copy(prim_hbm, prim, load_sem.at[1])
     load_obj = pltpu.make_async_copy(obj_hbm, out, load_sem.at[2])
+    load_height = pltpu.make_async_copy(height_hbm, height_ref, load_sem.at[3])
+    load_small = [
+        pltpu.make_async_copy(shock_hbm, shock_ref, load_sem.at[4]),
+        pltpu.make_async_copy(by_height_hbm, by_height_ref, load_sem.at[5]),
+        pltpu.make_async_copy(by_slope_hbm, by_slope_ref, load_sem.at[6]),
+        pltpu.make_async_copy(fitted_hbm, fitted_ref, load_sem.at[7]),
+    ]
+    load_height.start()
     load_psi.start()
     load_prim.start()
-    load_obj.start()
 
     barrier = pltpu.get_barrier_semaphore()
     for step in range(1, n_su):
@@ -117,6 +125,10 @@
     edge = remote(edge_send, edge_recv, 6, {"nrm": 1 - nrm})
     half = remote(half_send, half_recv, 7, {"nrm": 1 - nrm})
 
+    for load in load_small:
+        load.start()
+    load_obj.start()
+
     lane = lax.broadcasted_iota(jnp.int32, (1, LANES), 1)
     total_depth = 2 * LANES
     place = (nrm * LANES + lane).astype(jnp.float32)
@@ -134,9 +146,17 @@
         0.0,
     )
 
+    load_height.wait()
     turn[...] = jnp.zeros_like(turn)
     turn[0:rows, 0:cols] = 1.0 / height_ref[...]
     height_t[...] = turn[...].T[0:cols]
+
+    def widen(row, carry):
+        column = pltpu.roll(height_t[...], LANES - row, 1)[:, 0:1]
+        height_wide[row] = jnp.broadcast_to(column, (cols, LANES))
+        return carry
+
+    lax.fori_loop(0, rows, widen, 0, unroll=4)
 
     @pl.when(su == 0)
     def _():
@@ -179,7 +199,7 @@
         return (top, bottom)
 
     blank = jnp.zeros((cols, LANES), jnp.float32)
-    top, bottom = lax.fori_loop(0, rows, pack, (blank, blank))
+    top, bottom = lax.fori_loop(0, rows, pack, (blank, blank), unroll=4)
     top_pack[...] = top
     edge_send[...] = jnp.where(nrm == 0, top, pltpu.roll(bottom, LANES - 1, 1))
     edge.start()
@@ -205,7 +225,7 @@
         sv_send[1, 5, row] = rad_v[row, SUB + cols - 2 : SUB + cols, :]
         return carry
 
-    lax.fori_loop(0, rows, radii, 0)
+    lax.fori_loop(0, rows, radii, 0, unroll=2)
 
     @pl.when(sv > 0)
     def _():
@@ -226,13 +246,12 @@
     edge.wait_recv()
 
     def metric_row(row, sums):
-        scale = pltpu.roll(height_t[...], LANES - row, 1)[:, 0:1]
         pieces = []
         for chunk in range(chunks):
             part = slice(chunk * SUB, chunk * SUB + SUB)
             state = [prim[comp, row, part, :] for comp in range(5)]
             flux = line_flux(state, enth[row, part, :])
-            factor = jnp.broadcast_to(scale[part], (SUB, LANES))
+            factor = height_wide[row, part, :]
             total = None
             for comp in range(5):
                 value = psi[comp, row + 2, SUB + chunk * SUB : 2 * SUB + chunk * SUB, :]
@@ -248,8 +267,10 @@
             pieces.append(jnp.sum(total, axis=1, keepdims=True))
         return jnp.where(lane == row, jnp.concatenate(pieces, 0), sums)
 
-    sums = lax.fori_loop(0, rows, metric_row, blank)
-
+    sums = lax.fori_loop(0, rows, metric_row, blank, unroll=4)
+
+    for load in load_small:
+        load.wait()
     turn[...] = jnp.zeros_like(turn)
     turn[0:cols, :] = sums
     line_sums = turn[...].T[0:rows, 0:cols]
@@ -292,7 +313,7 @@
         rad_v[row, SUB + cols : SUB + cols + 2, :] = sv_recv[1, 5, row]
         return carry
 
-    lax.fori_loop(0, rows, unpack, 0)
+    lax.fori_loop(0, rows, unpack, 0, unroll=4)
     load_obj.wait()
 
     def residual_row(row, carry):
@@ -407,25 +428,6 @@
     turn[0:rows, 0:cols] = slope
     slope_t[...] = turn[...].T[0:cols]
 
-    def store(row):
-        return pltpu.make_async_copy(
-            out.at[:, pl.ds(row, 1)], out_hbm.at[:, pl.ds(row, 1)], store_sem.at[row]
-        )
-
-    def slope_row(row, carry):
-        column = pltpu.roll(slope_t[...], LANES - row, 1)[:, 0:1]
-        for chunk in range(chunks):
-            part = slice(chunk * SUB, chunk * SUB + SUB)
-            state = [prim[comp, row, part, :] for comp in range(5)]
-            flux = line_flux(state, enth[row, part, :])
-            weight = jnp.broadcast_to(column[part], (SUB, LANES)) * fraction
-            for comp in range(5):
-                out[comp, row, part, :] = out[comp, row, part, :] + weight * flux[comp]
-        store(row).start()
-        return carry
-
-    lax.fori_loop(0, rows, slope_row, 0)
-
     @pl.when(su > 0)
     def _():
         psi_down.wait_send()
@@ -451,11 +453,34 @@
         def _(other=other):
             total_copy(su, other).wait_send()
 
-    def finish(row, carry):
-        store(row).wait()
-        return carry
-
-    lax.fori_loop(0, rows, finish, 0)
+
+def finish_kernel(part_ref, prim, enth, slope_ref, slope_t, out_hbm, slope_hbm, out, sem, slope_sem):
+    rows, cols = prim.shape[1], prim.shape[2]
+    nrm = lax.axis_index("nrm")
+    store_slope = pltpu.make_async_copy(slope_ref, slope_hbm, slope_sem)
+    store_slope.start()
+    lane = lax.broadcasted_iota(jnp.int32, (1, LANES), 1)
+    fraction = ((nrm * LANES + lane).astype(jnp.float32) + 0.5) / (2 * LANES)
+    group = 4
+
+    def store(lap):
+        where = pl.ds(lap * group, group)
+        return pltpu.make_async_copy(out.at[:, where], out_hbm.at[:, where], sem.at[lap])
+
+    for lap in range(rows // group):
+        for row in range(lap * group, lap * group + group):
+            column = jnp.broadcast_to(slope_t[:, row : row + 1], (cols, LANES))
+            for chunk in range(cols // SUB):
+                part = slice(chunk * SUB, chunk * SUB + SUB)
+                state = [prim[comp, row, part, :] for comp in range(5)]
+                flux = line_flux(state, enth[row, part, :])
+                weight = column[part] * fraction
+                for comp in range(5):
+                    out[comp, row, part, :] = part_ref[comp, row, part, :] + weight * flux[comp]
+        store(lap).start()
+    for lap in range(rows // group):
+        store(lap).wait()
+    store_slope.wait()
 
 
 def local(
@@ -466,26 +491,40 @@
     _, rows, cols, depth = primitive.shape
     f32 = jnp.float32
     vmem = pl.BlockSpec(memory_space=pltpu.VMEM)
-    hbm = pl.BlockSpec(memory_space=pl.ANY)
     block = (5, rows, cols, depth)
     wide = cols + 2 * SUB
     dma = pltpu.SemaphoreType.DMA
-    return pl.pallas_call(
+    operands = [
+        pltpu.with_memory_space_constraint(operand, pltpu.HBM)
+        for operand in (
+            front_height, shock_state, state_by_height, state_by_slope, fitted_flags,
+            primitive, adjoint_state, objective_grad,
+        )
+    ]
+    small = (5, rows, cols)
+    hbm = pl.BlockSpec(memory_space=pltpu.HBM)
+    shape = jax.ShapeDtypeStruct
+    held = pl.pallas_call(
         functools.partial(kernel, n_su, n_sv),
         out_shape=(
-            jax.ShapeDtypeStruct(block, f32),
-            jax.ShapeDtypeStruct((rows, cols), f32),
+            shape(block, f32),
+            shape(block, f32),
+            shape((rows, cols, depth), f32),
+            shape((rows, cols), f32),
+            shape((cols, LANES), f32),
         ),
-        in_specs=[vmem] * 5 + [hbm] * 3,
-        out_specs=(hbm, vmem),
+        in_specs=[hbm] * 8,
+        out_specs=[vmem] * 5,
         scratch_shapes=[
             pltpu.VMEM((5, rows + 4, wide, depth), f32),
             pltpu.VMEM(block, f32),
-            pltpu.VMEM(block, f32),
-            pltpu.VMEM(block, f32),
-            pltpu.VMEM((rows, cols, depth), f32),
             pltpu.VMEM((rows + 4, cols, depth), f32),
             pltpu.VMEM((rows, wide, depth), f32),
+            pltpu.VMEM((rows, cols), f32),
+            pltpu.VMEM(small, f32),
+            pltpu.VMEM(small, f32),
+            pltpu.VMEM(small, f32),
+            pltpu.VMEM((rows, cols), jnp.int32),
             pltpu.VMEM((2, 6, rows, 2, depth), f32),
             pltpu.VMEM((2, 6, rows, 2, depth), f32),
             pltpu.VMEM((cols, LANES), f32),
@@ -493,25 +532,29 @@
             pltpu.VMEM((cols, LANES), f32),
             pltpu.VMEM((LANES, LANES), f32),
             pltpu.VMEM((cols, LANES), f32),
-            pltpu.VMEM((cols, LANES), f32),
+            pltpu.VMEM((rows, cols, LANES), f32),
             pltpu.VMEM((2, rows, LANES), f32),
             pltpu.VMEM((2, rows, LANES), f32),
             pltpu.VMEM((1, LANES), f32),
             pltpu.VMEM((n_su, 1, LANES), f32),
-            dma((3,)),
-            dma((rows,)),
+            dma((8,)),
             dma((8,)),
             dma((8,)),
             dma((n_su,)),
             dma((n_su,)),
         ],
         compiler_params=pltpu.CompilerParams(
-            collective_id=0, has_side_effects=True, vmem_limit_bytes=40 * 1024 * 1024
+            collective_id=0, has_side_effects=True, vmem_limit_bytes=24 * 1024 * 1024
         ),
-    )(
-        front_height, shock_state, state_by_height, state_by_slope, fitted_flags,
-        primitive, adjoint_state, objective_grad,
-    )
+    )(*operands)
+    return pl.pallas_call(
+        finish_kernel,
+        out_shape=(shape(block, f32), shape((rows, cols), f32)),
+        in_specs=[vmem] * 5,
+        out_specs=(hbm, hbm),
+        scratch_shapes=[pltpu.VMEM(block, f32), dma((rows // 4,)), dma],
+        compiler_params=pltpu.CompilerParams(vmem_limit_bytes=16 * 1024 * 1024),
+    )(*held)
 
 
 def solution(mesh):

time: 35.3 us -> 23.5 us (0.67)
  local copies, waits for them, and re-layouts: 9.77 us -> 0 us
  Pallas kernels: 24.4 us -> 22.6 us
    unnamed x18 -> x0, local copies, waits for them, and re-layouts: 9.77 us -> none
    pallas_call x1 -> x2, Pallas kernels: 24.4 us -> 22.6 us  [the longest x1 21.3 us: local(): pl.pallas_call(functools.partial(kernel, n_su, n_sv), out_shape=(shape(bl...]
where the time goes in v2:
time: 23.5 us; the launch traced here: 23.3 us
  Pallas kernels  22.6 us (96%)
  between operations  0.64 us (3%)
    pallas_call x1, Pallas kernels, local(): pl.pallas_call(functools.partial(kernel, n_su, n_sv), out_shape=(shape(bl...  21.3 us
    pallas_call x1, Pallas kernels, local(): pl.pallas_call(finish_kernel, out_shape=(shape(block, f32), shape((rows,...  1.33 us

profile of v2, /device:TPU:0, one launch (start us, length us, event | category | flops | bytes accessed | tf_op | source)
XLA Modules:
  0.0 23.3 jit_solution(12463643734895042982)
XLA Ops:
  0.6 21.3 %shard_map.95 = (f32[5,16,40,128]{3,2,1,0:T(8,128)S(1)}, f32[5,16,40,128]{3,2,1,0:T(8,128)S(1)}, f32[16,40,128]{2,1,0:T(8,128)S(1)}, f32[16,40]{1,0:T(8,128)S(1)}, f32[40,128]{1,0:T(8,128)S(1)}) custom-call(f32[16,40]{1,0:T(8,128)} %height_hbm.1, f32[5,16,40]{2,1,0:T(8,128)} %shock_hbm.1, f32[5,16,40]{2,1,0:T(8,128)} %by_height_hbm.1, ...), custom_call_target="tpu_custom_call" | custom-call | tf_op jit(solution)/shard_map/pallas_call | solution.py:507
  21.9 1.3 %shard_map.96 = (f32[5,16,40,128]{3,2,1,0:T(8,128)}, f32[16,40]{1,0:T(8,128)}) custom-call(f32[5,16,40,128]{3,2,1,0:T(8,128)S(1)} %get-tuple-element.7.part_ref, f32[5,16,40,128]{3,2,1,0:T(8,128)S(1)} %get-tuple-element.8.prim, f32[16,40,128]{2,1,0:T(8,128)S(1)} %get-tuple-element.9.enth, f32[16,40]{1,0:T(8,128)S(1)} %get-tuple-element.10.slope_ref, ...), custom_call_target="tpu_custom_call" | custom-call | tf_op jit(solution)/shard_map/pallas_call | solution.py:550

commit v3 on v2

--- a/solution.py
+++ b/solution.py
@@ -88,10 +88,18 @@
     load_prim.start()
 
     barrier = pltpu.get_barrier_semaphore()
-    for step in range(1, n_su):
-        pl.semaphore_signal(
-            barrier, inc=1, device_id={"su": lax.rem(su + step, n_su)}, device_id_type=MESH
-        )
+    for other in range(1, n_su):
+        @pl.when(other > su)
+        def _(other=other):
+            for side in range(2):
+                pl.semaphore_signal(
+                    barrier, inc=1, device_id={"su": other, "nrm": side}, device_id_type=MESH
+                )
+
+    @pl.when(su > 0)
+    def _():
+        pl.semaphore_signal(barrier, inc=1, device_id={"su": su - 1}, device_id_type=MESH)
+
     pl.semaphore_signal(barrier, inc=1, device_id={"nrm": 1 - nrm}, device_id_type=MESH)
 
     @pl.when(sv > 0)
@@ -176,7 +184,13 @@
     def _():
         sv_recv[1] = jnp.zeros((6, rows, 2, LANES), jnp.float32)
 
-    neighbours = n_su + (sv > 0).astype(jnp.int32) + (sv < n_sv - 1).astype(jnp.int32)
+    neighbours = (
+        2 * su
+        + 1
+        + (su < n_su - 1).astype(jnp.int32)
+        + (sv > 0).astype(jnp.int32)
+        + (sv < n_sv - 1).astype(jnp.int32)
+    )
     pl.semaphore_wait(barrier, neighbours)
 
     @pl.when(su > 0)
@@ -242,6 +256,30 @@
     @pl.when(su < n_su - 1)
     def _():
         rad_up.start()
+
+    for load in load_small:
+        load.wait()
+    turn[...] = jnp.zeros_like(turn)
+    turn[0:cols, :] = top_pack[...]
+    tops = turn[...].T
+    inverse = 1.0 / height_ref[...]
+    last = 0.5 * math.exp(stretch_rate * 0.5 / total_depth)
+    top_scaled = [
+        tops[comp * rows : comp * rows + rows, 0:cols] * (last * inverse) for comp in range(5)
+    ]
+    shock = [shock_ref[comp] for comp in range(5)]
+    shock_kinetic, shock_enthalpy = thermo(shock)
+    shock_flux = line_flux(shock, shock_enthalpy)
+    shock_adjoint = flux_transpose_normal(shock, shock_kinetic, shock_enthalpy, top_scaled)
+    fitted = fitted_ref[...].astype(jnp.float32)
+    front_flux = sum(top_scaled[comp] * shock_flux[comp] for comp in range(5))
+    front_height = fitted * sum(shock_adjoint[comp] * by_height_ref[comp] for comp in range(5))
+    front_slope = fitted * sum(shock_adjoint[comp] * by_slope_ref[comp] for comp in range(5))
+    on_front = nrm == 1
+    half_send[...] = jnp.zeros_like(half_send)
+    half_send[0, :, 0:cols] = jnp.where(on_front, front_height - front_flux * inverse, 0.0)
+    half_send[1, :, 0:cols] = jnp.where(on_front, front_slope, 0.0)
+    tot_send[...] = jnp.zeros_like(tot_send)
 
     edge.wait_recv()
 
@@ -269,32 +307,28 @@
 
     sums = lax.fori_loop(0, rows, metric_row, blank, unroll=4)
 
-    for load in load_small:
-        load.wait()
     turn[...] = jnp.zeros_like(turn)
     turn[0:cols, :] = sums
-    line_sums = turn[...].T[0:rows, 0:cols]
-    turn[0:cols, :] = top_pack[...]
-    tops = turn[...].T
-    inverse = 1.0 / height_ref[...]
-    last = 0.5 * math.exp(stretch_rate * 0.5 / total_depth)
-    top_scaled = [
-        tops[comp * rows : comp * rows + rows, 0:cols] * (last * inverse) for comp in range(5)
-    ]
-    shock = [shock_ref[comp] for comp in range(5)]
-    shock_kinetic, shock_enthalpy = thermo(shock)
-    shock_flux = line_flux(shock, shock_enthalpy)
-    shock_adjoint = flux_transpose_normal(shock, shock_kinetic, shock_enthalpy, top_scaled)
-    fitted = fitted_ref[...].astype(jnp.float32)
-    front_flux = sum(top_scaled[comp] * shock_flux[comp] for comp in range(5))
-    front_height = fitted * sum(shock_adjoint[comp] * by_height_ref[comp] for comp in range(5))
-    front_slope = fitted * sum(shock_adjoint[comp] * by_slope_ref[comp] for comp in range(5))
-    on_front = nrm == 1
-    half_send[...] = jnp.zeros_like(half_send)
-    half_send[0, :, 0:cols] = (
-        jnp.where(on_front, front_height - front_flux * inverse, 0.0) - line_sums * inverse
-    )
-    half_send[1, :, 0:cols] = jnp.where(on_front, front_slope, 0.0)
+    part_height = half_send[0, :, 0:cols] - turn[...].T[0:rows, 0:cols] / height_ref[...]
+    tot_send[:, 0:cols] = jnp.sum(part_height, axis=0, keepdims=True)
+
+    def total_copy(source, source_side, dest, dest_side):
+        return pltpu.make_async_remote_copy(
+            src_ref=tot_send,
+            dst_ref=tot_recv.at[source_side * n_su + source],
+            send_sem=tot_ssem.at[dest_side * n_su + dest],
+            recv_sem=tot_rsem.at[source_side * n_su + source],
+            device_id={"su": dest, "nrm": dest_side},
+            device_id_type=MESH,
+        )
+
+    for other in range(n_su - 1):
+        @pl.when(other < su)
+        def _(other=other):
+            for side in range(2):
+                total_copy(su, nrm, other, side).start()
+
+    half_send[0, :, 0:cols] = part_height
     half.start()
 
     @pl.when(sv > 0)
@@ -369,8 +403,20 @@
             )
         return carry
 
-    middle = rows // 2
-    lax.fori_loop(2, middle, residual_row, 0)
+    lax.fori_loop(2, rows - 2, residual_row, 0)
+
+    @pl.when(su > 0)
+    def _():
+        psi_up.wait_recv()
+        rad_up.wait_recv()
+
+    @pl.when(su < n_su - 1)
+    def _():
+        psi_down.wait_recv()
+        rad_down.wait_recv()
+
+    lax.fori_loop(0, 2, residual_row, 0)
+    lax.fori_loop(rows - 2, rows, residual_row, 0)
 
     half.wait_recv()
     summed = half_send[0, :, 0:cols] + half_recv[0, :, 0:cols]
@@ -381,47 +427,17 @@
             [summed[step:], jnp.zeros((step, cols), jnp.float32)], 0
         )
         step *= 2
-    tot_send[...] = jnp.zeros_like(tot_send)
-    tot_send[:, 0:cols] = summed[0:1]
-
-    def total_copy(source, dest):
-        return pltpu.make_async_remote_copy(
-            src_ref=tot_send,
-            dst_ref=tot_recv.at[source],
-            send_sem=tot_ssem.at[dest],
-            recv_sem=tot_rsem.at[source],
-            device_id={"su": dest},
-            device_id_type=MESH,
-        )
-
-    for other in range(n_su - 1):
-        @pl.when(other < su)
-        def _(other=other):
-            total_copy(su, other).start()
-
-    lax.fori_loop(middle, rows - 2, residual_row, 0)
-
-    @pl.when(su > 0)
-    def _():
-        psi_up.wait_recv()
-        rad_up.wait_recv()
-
-    @pl.when(su < n_su - 1)
-    def _():
-        psi_down.wait_recv()
-        rad_down.wait_recv()
-
-    lax.fori_loop(0, 2, residual_row, 0)
-    lax.fori_loop(rows - 2, rows, residual_row, 0)
 
     for other in range(1, n_su):
         @pl.when(other > su)
         def _(other=other):
-            total_copy(other, su).wait_recv()
+            for side in range(2):
+                total_copy(other, side, su, nrm).wait_recv()
 
     upstream = jnp.zeros((1, cols), jnp.float32)
     for other in range(n_su - 1, 0, -1):
-        upstream = upstream + jnp.where(other > su, tot_recv[other, :, 0:cols], 0.0)
+        both = tot_recv[other, :, 0:cols] + tot_recv[n_su + other, :, 0:cols]
+        upstream = upstream + jnp.where(other > su, both, 0.0)
     slope = (summed + upstream) * (1.0 / (rows * n_su)) + front_slope
     slope_ref[...] = slope
     turn[...] = jnp.zeros_like(turn)
@@ -451,7 +467,8 @@
     for other in range(n_su - 1):
         @pl.when(other < su)
         def _(other=other):
-            total_copy(su, other).wait_send()
+            for side in range(2):
+                total_copy(su, nrm, other, side).wait_send()
 
 
 def finish_kernel(part_ref, prim, enth, slope_ref, slope_t, out_hbm, slope_hbm, out, sem, slope_sem):
@@ -536,12 +553,12 @@
             pltpu.VMEM((2, rows, LANES), f32),
             pltpu.VMEM((2, rows, LANES), f32),
             pltpu.VMEM((1, LANES), f32),
-            pltpu.VMEM((n_su, 1, LANES), f32),
+            pltpu.VMEM((2 * n_su, 1, LANES), f32),
             dma((8,)),
             dma((8,)),
             dma((8,)),
-            dma((n_su,)),
-            dma((n_su,)),
+            dma((2 * n_su,)),
+            dma((2 * n_su,)),
         ],
         compiler_params=pltpu.CompilerParams(
             collective_id=0, has_side_effects=True, vmem_limit_bytes=24 * 1024 * 1024

time: 23.5 us -> 21.3 us (0.906)
  Pallas kernels: 22.6 us -> 20.5 us
    pallas_call x1, Pallas kernels: 21.3 us -> 19.1 us  [local(): pl.pallas_call(functools.partial(kernel, n_su, n_sv), out_shape=(shape(bl...]
where the time goes in v3:
time: 21.3 us; the launch traced here: 21.1 us
  Pallas kernels  20.5 us (96%)
  between operations  0.64 us (3%)
    pallas_call x1, Pallas kernels, local(): pl.pallas_call(functools.partial(kernel, n_su, n_sv), out_shape=(shape(bl...  19.1 us
    pallas_call x1, Pallas kernels, local(): pl.pallas_call(finish_kernel, out_shape=(shape(block, f32), shape((rows,...  1.33 us

profile of v3, /device:TPU:0, one launch (start us, length us, event | category | flops | bytes accessed | tf_op | source)
XLA Modules:
  0.0 21.1 jit_solution(8165234926051793432)
XLA Ops:
  0.6 19.1 %shard_map.95 = (f32[5,16,40,128]{3,2,1,0:T(8,128)S(1)}, f32[5,16,40,128]{3,2,1,0:T(8,128)S(1)}, f32[16,40,128]{2,1,0:T(8,128)S(1)}, f32[16,40]{1,0:T(8,128)S(1)}, f32[40,128]{1,0:T(8,128)S(1)}) custom-call(f32[16,40]{1,0:T(8,128)} %height_hbm.1, f32[5,16,40]{2,1,0:T(8,128)} %shock_hbm.1, f32[5,16,40]{2,1,0:T(8,128)} %by_height_hbm.1, ...), custom_call_target="tpu_custom_call" | custom-call | tf_op jit(solution)/shard_map/pallas_call | solution.py:524
  19.8 1.3 %shard_map.96 = (f32[5,16,40,128]{3,2,1,0:T(8,128)}, f32[16,40]{1,0:T(8,128)}) custom-call(f32[5,16,40,128]{3,2,1,0:T(8,128)S(1)} %get-tuple-element.7.part_ref, f32[5,16,40,128]{3,2,1,0:T(8,128)S(1)} %get-tuple-element.8.prim, f32[16,40,128]{2,1,0:T(8,128)S(1)} %get-tuple-element.9.enth, f32[16,40]{1,0:T(8,128)S(1)} %get-tuple-element.10.slope_ref, ...), custom_call_target="tpu_custom_call" | custom-call | tf_op jit(solution)/shard_map/pallas_call | solution.py:567

commit v4 on v3

--- a/solution.py
+++ b/solution.py
@@ -72,10 +72,21 @@
     chunks = cols // SUB
     su, sv, nrm = lax.axis_index("su"), lax.axis_index("sv"), lax.axis_index("nrm")
     own = pl.ds(SUB, cols)
-
-    load_psi = pltpu.make_async_copy(psi_hbm, psi.at[:, pl.ds(2, rows), own], load_sem.at[0])
-    load_prim = pltpu.make_async_copy(prim_hbm, prim, load_sem.at[1])
-    load_obj = pltpu.make_async_copy(obj_hbm, out, load_sem.at[2])
+    origin = lax.div(nrm, 2)
+
+    load_psi, load_prim, load_obj = [], [], []
+    for comp in range(5):
+        load_psi.append(
+            pltpu.make_async_copy(
+                psi_hbm.at[comp], psi.at[comp, pl.ds(2, rows), own], load_sem.at[8 + comp]
+            )
+        )
+        load_prim.append(
+            pltpu.make_async_copy(prim_hbm.at[comp], prim.at[comp], load_sem.at[13 + comp])
+        )
+        load_obj.append(
+            pltpu.make_async_copy(obj_hbm.at[comp], out.at[comp], load_sem.at[18 + comp])
+        )
     load_height = pltpu.make_async_copy(height_hbm, height_ref, load_sem.at[3])
     load_small = [
         pltpu.make_async_copy(shock_hbm, shock_ref, load_sem.at[4]),
@@ -84,8 +95,8 @@
         pltpu.make_async_copy(fitted_hbm, fitted_ref, load_sem.at[7]),
     ]
     load_height.start()
-    load_psi.start()
-    load_prim.start()
+    for load in load_psi + load_prim:
+        load.start()
 
     barrier = pltpu.get_barrier_semaphore()
     for other in range(1, n_su):
@@ -133,9 +144,8 @@
     edge = remote(edge_send, edge_recv, 6, {"nrm": 1 - nrm})
     half = remote(half_send, half_recv, 7, {"nrm": 1 - nrm})
 
-    for load in load_small:
+    for load in load_small + load_obj:
         load.start()
-    load_obj.start()
 
     lane = lax.broadcasted_iota(jnp.int32, (1, LANES), 1)
     total_depth = 2 * LANES
@@ -201,7 +211,8 @@
     def _():
         psi_up.start()
 
-    load_psi.wait()
+    for load in load_psi:
+        load.wait()
 
     def pack(row, carry):
         top, bottom = carry
@@ -218,7 +229,8 @@
     edge_send[...] = jnp.where(nrm == 0, top, pltpu.roll(bottom, LANES - 1, 1))
     edge.start()
 
-    load_prim.wait()
+    for load in load_prim:
+        load.wait()
 
     def radii(row, carry):
         for chunk in range(chunks):
@@ -312,6 +324,9 @@
     part_height = half_send[0, :, 0:cols] - turn[...].T[0:rows, 0:cols] / height_ref[...]
     tot_send[:, 0:cols] = jnp.sum(part_height, axis=0, keepdims=True)
 
+    half_send[0, :, 0:cols] = part_height
+    half.start()
+
     def total_copy(source, source_side, dest, dest_side):
         return pltpu.make_async_remote_copy(
             src_ref=tot_send,
@@ -328,9 +343,6 @@
             for side in range(2):
                 total_copy(su, nrm, other, side).start()
 
-    half_send[0, :, 0:cols] = part_height
-    half.start()
-
     @pl.when(sv > 0)
     def _():
         sv_up.wait_recv()
@@ -348,7 +360,8 @@
         return carry
 
     lax.fori_loop(0, rows, unpack, 0, unroll=4)
-    load_obj.wait()
+    for load in load_obj:
+        load.wait()
 
     def residual_row(row, carry):
         for chunk in range(chunks):
@@ -358,14 +371,16 @@
             density, u1, u2, u3, pressure = [prim[comp, row, part, :] for comp in range(5)]
             enthalpy = enth[row, part, :]
             ru = [rad_u[row + offset, part, :] for offset in range(5)]
-            rv = [rad_v[row, wide.start + offset - 2 : wide.stop + offset - 2, :] for offset in range(5)]
+            rv = [
+                rad_v[row, pl.ds(wide.start + offset - 2 + origin, SUB), :] for offset in range(5)
+            ]
             ruv = 6.0 * (ru[2] + rv[2])
             g1, g2, damped = [], [], []
             for comp in range(5):
                 centre = psi[comp, row + 2, wide, :]
                 along = [psi[comp, row + offset, wide, :] for offset in (0, 1, 3, 4)]
                 across = [
-                    psi[comp, row + 2, wide.start + offset : wide.stop + offset, :]
+                    psi[comp, row + 2, pl.ds(wide.start + offset + origin, SUB), :]
                     for offset in (-2, -1, 1, 2)
                 ]
                 g1.append((along[1] - along[2]) * (2.0 / 3.0) - (along[0] - along[3]) * (1.0 / 12.0))
@@ -554,7 +569,7 @@
             pltpu.VMEM((2, rows, LANES), f32),
             pltpu.VMEM((1, LANES), f32),
             pltpu.VMEM((2 * n_su, 1, LANES), f32),
-            dma((8,)),
+            dma((23,)),
             dma((8,)),
             dma((8,)),
             dma((2 * n_su,)),

time: 21.3 us -> 21.5 us (level)
  no operation moved by 1% of the time
where the time goes in v4:
time: 21.5 us; the launch traced here: 21.3 us
  Pallas kernels  20.6 us (96%)
  between operations  0.64 us (3%)
    pallas_call x1, Pallas kernels, local(): pl.pallas_call(functools.partial(kernel, n_su, n_sv), out_shape=(shape(bl...  19.3 us
    pallas_call x1, Pallas kernels, local(): pl.pallas_call(finish_kernel, out_shape=(shape(block, f32), shape((rows,...  1.33 us

profile of v4, /device:TPU:0, one launch (start us, length us, event | category | flops | bytes accessed | tf_op | source)
XLA Modules:
  0.0 21.3 jit_solution(5506081415194767595)
XLA Ops:
  0.6 19.3 %shard_map.95 = (f32[5,16,40,128]{3,2,1,0:T(8,128)S(1)}, f32[5,16,40,128]{3,2,1,0:T(8,128)S(1)}, f32[16,40,128]{2,1,0:T(8,128)S(1)}, f32[16,40]{1,0:T(8,128)S(1)}, f32[40,128]{1,0:T(8,128)S(1)}) custom-call(f32[16,40]{1,0:T(8,128)} %height_hbm.1, f32[5,16,40]{2,1,0:T(8,128)} %shock_hbm.1, f32[5,16,40]{2,1,0:T(8,128)} %by_height_hbm.1, ...), custom_call_target="tpu_custom_call" | custom-call | tf_op jit(solution)/shard_map/pallas_call | solution.py:539
  19.9 1.3 %shard_map.96 = (f32[5,16,40,128]{3,2,1,0:T(8,128)}, f32[16,40]{1,0:T(8,128)}) custom-call(f32[5,16,40,128]{3,2,1,0:T(8,128)S(1)} %get-tuple-element.7.part_ref, f32[5,16,40,128]{3,2,1,0:T(8,128)S(1)} %get-tuple-element.8.prim, f32[16,40,128]{2,1,0:T(8,128)S(1)} %get-tuple-element.9.enth, f32[16,40]{1,0:T(8,128)S(1)} %get-tuple-element.10.slope_ref, ...), custom_call_target="tpu_custom_call" | custom-call | tf_op jit(solution)/shard_map/pallas_call | solution.py:582

commit v5 on v3

--- a/solution.py
+++ b/solution.py
@@ -64,7 +64,7 @@
     out, prim, enth, slope_ref, slope_t,
     psi, normal, rad_u, rad_v,
     height_ref, shock_ref, by_height_ref, by_slope_ref, fitted_ref,
-    sv_send, sv_recv, edge_send, edge_recv, top_pack, turn, height_t, height_wide,
+    sv_send, sv_recv, edge_send, edge_recv, top_pack, turn, height_t, height_wide, band, line_terms,
     half_send, half_recv, tot_send, tot_recv,
     load_sem, send_sem, recv_sem, tot_ssem, tot_rsem,
 ):
@@ -145,8 +145,12 @@
     def half_inverse(position):
         return 0.5 * jnp.exp(stretch_rate * (1.0 - (position + 0.5) / total_depth))
 
-    below = jnp.where(lane == 0, 0.0, half_inverse(place - 1.0))
-    above = jnp.where(lane == LANES - 1, 0.0, half_inverse(place + 1.0))
+    own_weight = half_inverse(place)
+    source = lax.rem(lax.broadcasted_iota(jnp.int32, (2 * LANES, LANES), 0), LANES)
+    column = lax.broadcasted_iota(jnp.int32, (2 * LANES, LANES), 1)
+    band[...] = (source == column - 1).astype(jnp.float32) - (source == column + 1).astype(
+        jnp.float32
+    )
     target = jnp.where(nrm == 0, LANES - 1, 0)
     edge_weight = jnp.where(
         lane == target,
@@ -283,29 +287,50 @@
 
     edge.wait_recv()
 
-    def metric_row(row, sums):
-        pieces = []
-        for chunk in range(chunks):
-            part = slice(chunk * SUB, chunk * SUB + SUB)
-            state = [prim[comp, row, part, :] for comp in range(5)]
-            flux = line_flux(state, enth[row, part, :])
-            factor = height_wide[row, part, :]
+    group = 4
+
+    def split(value):
+        coarse = value.astype(jnp.bfloat16).astype(jnp.float32)
+        return jnp.concatenate([coarse, value - coarse], 1)
+
+    def metric_rows(lap, carry):
+        first = lap * group
+        lines = [
+            psi[comp, first + step + 2, SUB : SUB + cols, :] * own_weight
+            for step in range(group)
+            for comp in range(5)
+        ]
+        differences = jnp.dot(
+            split(jnp.concatenate(lines, 0)), band[...], preferred_element_type=jnp.float32
+        )
+        for step in range(group):
+            row = first + step
+            state = [prim[comp, row] for comp in range(5)]
+            flux = line_flux(state, enth[row])
+            factor = height_wide[row]
             total = None
             for comp in range(5):
-                value = psi[comp, row + 2, SUB + chunk * SUB : 2 * SUB + chunk * SUB, :]
+                start = (step * 5 + comp) * cols
                 shift = lax.rem(target - (comp * rows + row) + LANES, LANES)
                 difference = (
-                    pltpu.roll(value, 1, 1) * below
-                    - pltpu.roll(value, LANES - 1, 1) * above
-                    + pltpu.roll(edge_recv[part, :], shift, 1) * edge_weight
+                    differences[start : start + cols]
+                    + pltpu.roll(edge_recv[...], shift, 1) * edge_weight
                 ) * factor
-                normal[comp, row, part, :] = difference
+                normal[comp, row] = difference
                 term = flux[comp] * difference
                 total = term if total is None else total + term
-            pieces.append(jnp.sum(total, axis=1, keepdims=True))
-        return jnp.where(lane == row, jnp.concatenate(pieces, 0), sums)
-
-    sums = lax.fori_loop(0, rows, metric_row, blank, unroll=4)
+            line_terms[row] = total
+        return carry
+
+    lax.fori_loop(0, rows // group, metric_rows, 0)
+    every = jnp.dot(
+        split(line_terms[...].reshape(rows * cols, LANES)),
+        jnp.ones((2 * LANES, LANES), jnp.float32),
+        preferred_element_type=jnp.float32,
+    )
+    sums = blank
+    for row in range(rows):
+        sums = jnp.where(lane == row, every[row * cols : row * cols + cols], sums)
 
     turn[...] = jnp.zeros_like(turn)
     turn[0:cols, :] = sums
@@ -550,6 +575,8 @@
             pltpu.VMEM((LANES, LANES), f32),
             pltpu.VMEM((cols, LANES), f32),
             pltpu.VMEM((rows, cols, LANES), f32),
+            pltpu.VMEM((2 * LANES, LANES), f32),
+            pltpu.VMEM((rows, cols, LANES), f32),
             pltpu.VMEM((2, rows, LANES), f32),
             pltpu.VMEM((2, rows, LANES), f32),
             pltpu.VMEM((1, LANES), f32),

time: 21.3 us -> 16.5 us (0.77)
  Pallas kernels: 20.5 us -> 15.6 us
    pallas_call x1, Pallas kernels: 19.1 us -> 14.3 us  [local(): pl.pallas_call(functools.partial(kernel, n_su, n_sv), out_shape=(shape(bl...]
where the time goes in v5:
time: 16.5 us; the launch traced here: 16.3 us
  Pallas kernels  15.6 us (95%)
  between operations  0.64 us (4%)
    pallas_call x1, Pallas kernels, local(): pl.pallas_call(functools.partial(kernel, n_su, n_sv), out_shape=(shape(bl...  14.3 us
    pallas_call x1, Pallas kernels, local(): pl.pallas_call(finish_kernel, out_shape=(shape(block, f32), shape((rows,...  1.33 us

profile of v5, /device:TPU:0, one launch (start us, length us, event | category | flops | bytes accessed | tf_op | source)
XLA Modules:
  0.0 16.3 jit_solution(519600489115423893)
XLA Ops:
  0.6 14.3 %shard_map.95 = (f32[5,16,40,128]{3,2,1,0:T(8,128)S(1)}, f32[5,16,40,128]{3,2,1,0:T(8,128)S(1)}, f32[16,40,128]{2,1,0:T(8,128)S(1)}, f32[16,40]{1,0:T(8,128)S(1)}, f32[40,128]{1,0:T(8,128)S(1)}) custom-call(f32[16,40]{1,0:T(8,128)} %height_hbm.1, f32[5,16,40]{2,1,0:T(8,128)} %shock_hbm.1, f32[5,16,40]{2,1,0:T(8,128)} %by_height_hbm.1, ...), custom_call_target="tpu_custom_call" | custom-call | tf_op jit(solution)/shard_map/pallas_call | solution.py:549
  15.0 1.3 %shard_map.96 = (f32[5,16,40,128]{3,2,1,0:T(8,128)}, f32[16,40]{1,0:T(8,128)}) custom-call(f32[5,16,40,128]{3,2,1,0:T(8,128)S(1)} %get-tuple-element.7.part_ref, f32[5,16,40,128]{3,2,1,0:T(8,128)S(1)} %get-tuple-element.8.prim, f32[16,40,128]{2,1,0:T(8,128)S(1)} %get-tuple-element.9.enth, f32[16,40]{1,0:T(8,128)S(1)} %get-tuple-element.10.slope_ref, ...), custom_call_target="tpu_custom_call" | custom-call | tf_op jit(solution)/shard_map/pallas_call | solution.py:594
